TPU v7x, 32 devices: a whole 2x2x4 slice. The times are simulated.
32 devices in a mesh: tensor: 2 (over x), ctx: 4 (over z), dp: 4 (over y, core).
Axes of the slice: x: 2, y: 2, z: 4, core: 2. Of those that a mesh axis runs over, the one named last changes fastest.
Arguments:
- states: bfloat16 [4, 512, 2048], P('dp', 'ctx'), may hold values from -6 to 6
- lengths: int32 [4], P('dp'), may hold values from 1 to 512, 1280 in all
- first_gain: bfloat16 [2048], P(('ctx', 'dp')), may hold values from 0.25 to 1.75
- w_query: bfloat16 [2048, 2048], P(('ctx', 'dp'), 'tensor'), may hold values from -0.125 to 0.125
- key_matrix: bfloat16 [2048, 256], P(('ctx', 'dp'), 'tensor'), may hold values from -0.125 to 0.125
- value_matrix: bfloat16 [2048, 256], P(('ctx', 'dp'), 'tensor'), may hold values from -0.125 to 0.125
- w_out: bfloat16 [2048, 2048], P('tensor', ('ctx', 'dp')), may hold values from -1 to 1
- second_gain: bfloat16 [2048], P(('ctx', 'dp')), may hold values from 0.25 to 1.75
- w_gate: bfloat16 [2048, 5632], P(('ctx', 'dp'), 'tensor'), may hold values from -0.125 to 0.125
- w_up: bfloat16 [2048, 5632], P(('ctx', 'dp'), 'tensor'), may hold values from -0.125 to 0.125
- w_down: bfloat16 [5632, 2048], P('tensor', ('ctx', 'dp')), may hold values from -0.078125 to 0.078125
- cotangent: bfloat16 [4, 512, 2048], P('dp', 'ctx'), may hold values from -6 to 6
Outputs:
- layer_out: bfloat16 [4, 512, 2048], P('dp', 'ctx')
- grad_states: float32 [4, 512, 2048], P('dp', 'ctx')
- grad_first_gain: float32 [2048], P(('ctx', 'dp'))
- grad_query: float32 [2048, 2048], P(('ctx', 'dp'), 'tensor')
- grad_key: float32 [2048, 256], P(('ctx', 'dp'), 'tensor')
- grad_value: float32 [2048, 256], P(('ctx', 'dp'), 'tensor')
- grad_out: float32 [2048, 2048], P('tensor', ('ctx', 'dp'))
- grad_second_gain: float32 [2048], P(('ctx', 'dp'))
- grad_gate: float32 [2048, 5632], P(('ctx', 'dp'), 'tensor')
- grad_up: float32 [2048, 5632], P(('ctx', 'dp'), 'tensor')
- grad_down: float32 [5632, 2048], P('tensor', ('ctx', 'dp'))
Inputs may be any that keep to these rules, and one draw needn't show every extreme that they name: Slot s holds lengths[s] real tokens followed by padding; one slot is full, and the lengths add up to 1280.
All inputs are finite; a program needn't handle non-finite values. No bound on the sum of `lengths` on one device may be relied on, other than what follows from the above.
Results may differ from a plain program's by a relative error of at most 0.015.
Values may be sent and summed in bfloat16 or wider, within the bound.
A program may use at most 256 MiB of HBM per device.

v0:
```python
import jax
import jax.numpy as jnp
from jax import lax
from jax.sharding import PartitionSpec as P

HEAD_SIZE = 64


EPS = 1e-05
THETA = 10000.0
NEGATIVE = -1e30


def rope_tables(positions, half_width):
    inverse = jnp.exp(-jnp.log(THETA) * jnp.arange(half_width).astype(jnp.float32) / half_width)
    angles = positions.astype(jnp.float32)[:, None] * inverse[None, :]
    return (jnp.cos(angles)[:, None, :], jnp.sin(angles)[:, None, :])


def apply_rotation(vectors, cosine_table, sine_table):
    half_width = vectors.shape[-1] // 2
    first_half = vectors[..., :half_width]
    second_half = vectors[..., half_width:]
    return jnp.concatenate(
        [
            first_half * cosine_table - second_half * sine_table,
            second_half * cosine_table + first_half * sine_table,
        ],
        axis=-1,
    )


def rotate_back(grads, cosine_table, sine_table):
    half_width = grads.shape[-1] // 2
    first_half = grads[..., :half_width]
    second_half = grads[..., half_width:]
    return jnp.concatenate(
        [
            first_half * cosine_table + second_half * sine_table,
            second_half * cosine_table - first_half * sine_table,
        ],
        axis=-1,
    )


def times_transposed(left, right):
    return lax.dot_general(
        left, right, (((1,), (1,)), ((), ())), preferred_element_type=jnp.float32
    )


def transposed_times(left, right):
    return lax.dot_general(
        left, right, (((0,), (0,)), ((), ())), preferred_element_type=jnp.float32
    )


def norm_back(upstream, inputs, inverse_rms, gain):
    scaled = upstream * gain
    gain_grad = jnp.sum(upstream * inputs * inverse_rms, axis=0)
    inner = jnp.mean(scaled * inputs, axis=-1, keepdims=True)
    return (inverse_rms * scaled - inputs * inverse_rms**3 * inner, gain_grad)


def shards(
    states,
    lengths,
    first_gain,
    w_query,
    key_matrix,
    value_matrix,
    w_out,
    second_gain,
    w_gate,
    w_up,
    w_down,
    cotangent,
):
    low_type = jnp.bfloat16
    wide_type = jnp.float32
    gathered = (
        lax.all_gather(first_gain, ("ctx", "dp"), axis=0, tiled=True),
        lax.all_gather(w_query, ("ctx", "dp"), axis=0, tiled=True),
        lax.all_gather(key_matrix, ("ctx", "dp"), axis=0, tiled=True),
        lax.all_gather(value_matrix, ("ctx", "dp"), axis=0, tiled=True),
        lax.all_gather(w_out, ("ctx", "dp"), axis=1, tiled=True),
        lax.all_gather(second_gain, ("ctx", "dp"), axis=0, tiled=True),
        lax.all_gather(w_gate, ("ctx", "dp"), axis=0, tiled=True),
        lax.all_gather(w_up, ("ctx", "dp"), axis=0, tiled=True),
        lax.all_gather(w_down, ("ctx", "dp"), axis=1, tiled=True),
    )
    (
        gain_one,
        full_query,
        full_key,
        full_value,
        full_out,
        gain_two,
        full_gate,
        full_up,
        full_down,
    ) = gathered
    gain_one = gain_one.astype(wide_type)
    gain_two = gain_two.astype(wide_type)
    tokens = states.shape[1]
    inputs = states[0].astype(wide_type)
    seq_length = lengths[0]
    first_pos = lax.axis_index("ctx") * tokens
    positions = first_pos + jnp.arange(tokens, dtype=jnp.int32)
    cosine_table, sine_table = rope_tables(positions, HEAD_SIZE // 2)
    heads = full_query.shape[1] // HEAD_SIZE
    kv_heads = full_key.shape[1] // HEAD_SIZE
    group_factor = heads // kv_heads
    scale = HEAD_SIZE ** (-0.5)
    rms_one = lax.rsqrt(jnp.mean(inputs * inputs, axis=-1, keepdims=True) + EPS)
    first_normed = (inputs * rms_one * gain_one).astype(low_type)
    query_rows = jnp.dot(first_normed, full_query, preferred_element_type=wide_type)
    fresh_keys = jnp.dot(first_normed, full_key, preferred_element_type=wide_type)
    values_new = jnp.dot(first_normed, full_value, preferred_element_type=wide_type)
    query_rotated = (
        apply_rotation(query_rows.reshape(tokens, heads, HEAD_SIZE), cosine_table, sine_table)
        .astype(low_type)
        .reshape(tokens, kv_heads, group_factor, HEAD_SIZE)
    )
    key_rot = (
        apply_rotation(fresh_keys.reshape(tokens, kv_heads, HEAD_SIZE), cosine_table, sine_table)
        .astype(low_type)
        .reshape(tokens, kv_heads * HEAD_SIZE)
    )
    value_lower = values_new.astype(low_type)
    keys_all, values_all = (
        lax.all_gather(key_rot, "ctx", axis=0, tiled=True),
        lax.all_gather(value_lower, "ctx", axis=0, tiled=True),
    )
    total_keys = keys_all.shape[0]
    key_block = min(512, total_keys)
    block_count = total_keys // key_block

    def block_scores(begin_at):
        key_piece = lax.dynamic_slice_in_dim(keys_all, begin_at, key_block, 0).reshape(
            key_block, kv_heads, HEAD_SIZE
        )
        value_piece = lax.dynamic_slice_in_dim(values_all, begin_at, key_block, 0).reshape(
            key_block, kv_heads, HEAD_SIZE
        )
        scores = (
            jnp.einsum("qkgd,pkd->kgqp", query_rotated, key_piece, preferred_element_type=wide_type)
            * scale
        )
        key_pos = begin_at + jnp.arange(key_block, dtype=jnp.int32)
        allowed = (key_pos[None, :] <= positions[:, None]) & (key_pos[None, :] < seq_length)
        return (jnp.where(allowed, scores, NEGATIVE), key_piece, value_piece)

    def max_pass(index, carry):
        running, total = carry
        scores = block_scores(index * key_block)[0]
        newest = jnp.maximum(running, jnp.max(scores, axis=-1))
        total = total * jnp.exp(running - newest) + jnp.sum(
            jnp.exp(scores - newest[..., None]), axis=-1
        )
        return (newest, total)

    start_max = jnp.full((kv_heads, group_factor, tokens), NEGATIVE, wide_type)
    running, total = lax.fori_loop(0, block_count, max_pass, (start_max, jnp.zeros_like(start_max)))
    log_total = running + jnp.log(total)

    def mix_pass(index, carry):
        scores, key_piece, value_piece = block_scores(index * key_block)
        weights = jnp.exp(scores - log_total[..., None]).astype(low_type)
        return carry + jnp.einsum(
            "kgqp,pkd->qkgd", weights, value_piece, preferred_element_type=wide_type
        )

    mixed = lax.fori_loop(
        0, block_count, mix_pass, jnp.zeros((tokens, kv_heads, group_factor, HEAD_SIZE), wide_type)
    )
    mixed_low = mixed.reshape(tokens, heads * HEAD_SIZE).astype(low_type)
    attention = lax.psum(jnp.dot(mixed_low, full_out, preferred_element_type=wide_type), "tensor")
    hidden = inputs + attention
    rms_two = lax.rsqrt(jnp.mean(hidden * hidden, axis=-1, keepdims=True) + EPS)
    normed_two = (hidden * rms_two * gain_two).astype(low_type)
    gate = jnp.dot(normed_two, full_gate, preferred_element_type=wide_type)
    up_proj = jnp.dot(normed_two, full_up, preferred_element_type=wide_type)
    sigma = jax.nn.sigmoid(gate)
    swish = gate * sigma
    activated = (swish * up_proj).astype(low_type)
    branch = lax.psum(
        jnp.dot(activated, full_down, preferred_element_type=wide_type).astype(jnp.bfloat16),
        "tensor",
    ).astype(jnp.float32)
    layer_out = (hidden + branch).astype(low_type)
    valid = (positions < seq_length)[:, None]
    grad_y = jnp.where(valid, cotangent[0].astype(wide_type), 0.0)
    grad_y_low = grad_y.astype(low_type)
    grad_down = transposed_times(activated, grad_y_low)
    grad_act = times_transposed(grad_y_low, full_down)
    grad_gate_low = (grad_act * up_proj * (sigma * (1.0 + gate * (1.0 - sigma)))).astype(low_type)
    grad_up_low = (grad_act * swish).astype(low_type)
    grad_gate = transposed_times(normed_two, grad_gate_low)
    grad_up = transposed_times(normed_two, grad_up_low)
    grad_normed_two = lax.psum(
        times_transposed(grad_gate_low, full_gate) + times_transposed(grad_up_low, full_up),
        "tensor",
    )
    norm_part, grad_gain_two = norm_back(grad_normed_two, hidden, rms_two, gain_two)
    grad_hidden = grad_y + norm_part
    grad_hidden_low = grad_hidden.astype(low_type)
    grad_out = transposed_times(mixed_low, grad_hidden_low)
    grad_mixed = (
        times_transposed(grad_hidden_low, full_out)
        .astype(low_type)
        .reshape(tokens, kv_heads, group_factor, HEAD_SIZE)
    )

    def delta_pass(index, carry):
        scores, key_piece, value_piece = block_scores(index * key_block)
        probs = jnp.exp(scores - log_total[..., None])
        dprob = jnp.einsum(
            "qkgd,pkd->kgqp", grad_mixed, value_piece, preferred_element_type=wide_type
        )
        return carry + jnp.sum(probs * dprob, axis=-1)

    delta = lax.fori_loop(
        0, block_count, delta_pass, jnp.zeros((kv_heads, group_factor, tokens), wide_type)
    )

    def grad_pass(index, carry):
        grad_queries, key_grads, value_grads = carry
        begin_at = index * key_block
        scores, key_piece, value_piece = block_scores(begin_at)
        probs = jnp.exp(scores - log_total[..., None])
        dprob = jnp.einsum(
            "qkgd,pkd->kgqp", grad_mixed, value_piece, preferred_element_type=wide_type
        )
        grad_scores = (probs * (dprob - delta[..., None])).astype(low_type)
        grad_queries = (
            grad_queries
            + jnp.einsum("kgqp,pkd->qkgd", grad_scores, key_piece, preferred_element_type=wide_type)
            * scale
        )
        key_part = (
            jnp.einsum(
                "kgqp,qkgd->pkd", grad_scores, query_rotated, preferred_element_type=wide_type
            )
            * scale
        )
        value_part = jnp.einsum(
            "kgqp,qkgd->pkd", probs.astype(low_type), grad_mixed, preferred_element_type=wide_type
        )
        key_grads = lax.dynamic_update_slice_in_dim(
            key_grads, key_part.reshape(key_block, kv_heads * HEAD_SIZE), begin_at, 0
        )
        value_grads = lax.dynamic_update_slice_in_dim(
            value_grads, value_part.reshape(key_block, kv_heads * HEAD_SIZE), begin_at, 0
        )
        return (grad_queries, key_grads, value_grads)

    empty_keys = jnp.zeros((total_keys, kv_heads * HEAD_SIZE), wide_type)
    start_state = (
        jnp.zeros((tokens, kv_heads, group_factor, HEAD_SIZE), wide_type),
        empty_keys,
        empty_keys,
    )
    grad_queries, key_grads, value_grads = lax.fori_loop(0, block_count, grad_pass, start_state)
    key_local, value_local = (
        lax.psum_scatter(key_grads, "ctx", scatter_dimension=0, tiled=True),
        lax.psum_scatter(value_grads, "ctx", scatter_dimension=0, tiled=True),
    )
    grad_query_low = (
        rotate_back(grad_queries.reshape(tokens, heads, HEAD_SIZE), cosine_table, sine_table)
        .reshape(tokens, heads * HEAD_SIZE)
        .astype(low_type)
    )
    grad_key_low = (
        rotate_back(key_local.reshape(tokens, kv_heads, HEAD_SIZE), cosine_table, sine_table)
        .reshape(tokens, kv_heads * HEAD_SIZE)
        .astype(low_type)
    )
    grad_value_low = value_local.astype(low_type)
    grad_query = transposed_times(first_normed, grad_query_low)
    grad_key = transposed_times(first_normed, grad_key_low)
    grad_value = transposed_times(first_normed, grad_value_low)
    grad_normed_one = lax.psum(
        (
            times_transposed(grad_query_low, full_query)
            + times_transposed(grad_key_low, full_key)
            + times_transposed(grad_value_low, full_value)
        ).astype(jnp.bfloat16),
        "tensor",
    ).astype(jnp.float32)
    first_part, grad_gain_one = norm_back(grad_normed_one, inputs, rms_one, gain_one)
    grad_states = grad_hidden + first_part
    summed = tuple(
        (
            lax.psum_scatter(grad_gain_one, ("ctx", "dp"), scatter_dimension=0, tiled=True),
            lax.psum_scatter(grad_query, ("ctx", "dp"), scatter_dimension=0, tiled=True),
            lax.psum_scatter(grad_key, ("ctx", "dp"), scatter_dimension=0, tiled=True),
            lax.psum_scatter(grad_value, ("ctx", "dp"), scatter_dimension=0, tiled=True),
            lax.psum_scatter(grad_out, ("ctx", "dp"), scatter_dimension=1, tiled=True),
            lax.psum_scatter(grad_gain_two, ("ctx", "dp"), scatter_dimension=0, tiled=True),
            lax.psum_scatter(grad_gate, ("ctx", "dp"), scatter_dimension=0, tiled=True),
            lax.psum_scatter(grad_up, ("ctx", "dp"), scatter_dimension=0, tiled=True),
            lax.psum_scatter(grad_down, ("ctx", "dp"), scatter_dimension=1, tiled=True),
        )
    )
    return (
        layer_out[None],
        grad_states[None],
        summed[0],
        summed[1],
        summed[2],
        summed[3],
        summed[4],
        summed[5],
        summed[6],
        summed[7],
        summed[8],
    )


def solution(mesh):
    placed = (
        P("dp", "ctx", None),
        P("dp"),
        P(("ctx", "dp")),
        P(("ctx", "dp"), "tensor"),
        P(("ctx", "dp"), "tensor"),
        P(("ctx", "dp"), "tensor"),
        P("tensor", ("ctx", "dp")),
        P(("ctx", "dp")),
        P(("ctx", "dp"), "tensor"),
        P(("ctx", "dp"), "tensor"),
        P("tensor", ("ctx", "dp")),
        P("dp", "ctx", None),
    )
    return jax.shard_map(
        shards,
        mesh=mesh,
        in_specs=placed,
        out_specs=(
            P("dp", "ctx", None),
            P("dp", "ctx", None),
            P(("ctx", "dp")),
            P(("ctx", "dp"), "tensor"),
            P(("ctx", "dp"), "tensor"),
            P(("ctx", "dp"), "tensor"),
            P("tensor", ("ctx", "dp")),
            P(("ctx", "dp")),
            P(("ctx", "dp"), "tensor"),
            P(("ctx", "dp"), "tensor"),
            P("tensor", ("ctx", "dp")),
        ),
        check_vma=False,
    )
```

profile of v0, /device:TPU:8, one launch (start us, length us, event | category | flops | bytes accessed | tf_op | source)
XLA Modules:
  0.0 1652.8 jit_solution(8071266629286700061)
XLA Ops:
  8.7 18.9 %all-gather = bf16[16,1,128]{2,1,0:T(2,128)(2,1)S(1)} all-gather(bf16[1,1,128]{2,1,0:T(2,128)(2,1)} %bitcast.203), channel_id=1, replica_groups=mesh['tensor'=2,'ctx'=4,'dp'=4] {'ctx','dp'}, dimensions={0}, use_global_device_ids=true | all-gather | bytes 4352 | tf_op jit(solution)/shard_map/all_gather | solution.py:82
  29.4 20.7 %all_gather.34 = bf16[2048,128]{1,0:T(8,128)(2,1)S(1)} all-gather(bf16[128,128]{1,0:T(8,128)(2,1)} %param.17), channel_id=1, replica_groups=mesh['tensor'=2,'ctx'=4,'dp'=4] {'ctx','dp'}, dimensions={0}, use_global_device_ids=true | all-gather | bytes 557056 | tf_op jit(solution)/shard_map/all_gather | solution.py:85
  52.4 13.4 all_gather.35
  66.6 22.6 %all_gather.36 = bf16[2048,128]{1,0:T(8,128)(2,1)S(1)} all-gather(bf16[128,128]{1,0:T(8,128)(2,1)} %param.16), channel_id=1, replica_groups=mesh['tensor'=2,'ctx'=4,'dp'=4] {'ctx','dp'}, dimensions={0}, use_global_device_ids=true | all-gather | bytes 557056 | tf_op jit(solution)/shard_map/all_gather | solution.py:84
  90.0 14.4 all_gather.37
  104.6 6.5 copy.43
  127.7 16.4 all-gather.1
  144.1 20.8 %all-reduce.8.cloned.1.call-done = f32[128,2048]{1,0:T(8,128)} async-done(((f32[128,2048]{1,0:T(8,128)}), f32[128,2048]{1,0:T(8,128)}) %all-reduce.8.cloned.1.call-update) | async-done | bytes 1048592 | tf_op jit(solution)/shard_map/psum | solution.py:178
  166.5 94.0 %all-gather.12.cloned.1.call-done = bf16[2048,2816]{1,0:T(8,128)(2,1)} async-done(((bf16[128,2816]{1,0:T(8,128)(2,1)}), bf16[2048,2816]{1,0:T(8,128)(2,1)}) %all-gather.12.cloned.1.call-update) | async-done | bytes 11534352 | tf_op jit(solution)/shard_map/all_gather | solution.py:88
  260.4 7.0 fusion.70
  267.5 87.9 %all-gather.14.cloned.1.call-done = bf16[2048,2816]{1,0:T(8,128)(2,1)} async-done(((bf16[128,2816]{1,0:T(8,128)(2,1)}), bf16[2048,2816]{1,0:T(8,128)(2,1)}) %all-gather.14.cloned.1.call-update) | async-done | bytes 11534352 | tf_op jit(solution)/shard_map/all_gather | solution.py:89
  355.3 7.0 fusion.71
  362.4 90.1 %all-gather.16.cloned.1.call-done = bf16[2816,2048]{1,0:T(8,128)(2,1)} async-done(((bf16[2816,128]{1,0:T(8,128)(2,1)}), bf16[2816,2048]{1,0:T(8,128)(2,1)}) %all-gather.16.cloned.1.call-update) | async-done | bytes 11534352 | tf_op jit(solution)/shard_map/all_gather | solution.py:90
  452.5 9.4 multiply_convert_fusion
  461.9 8.8 fusion.72
  470.8 4.8 convolution_add_fusion.2
  475.9 6.7 convolution_convert_fusion
  482.6 33.2 %all-reduce.10.cloned.1.call-done = f32[128,2048]{1,0:T(8,128)} async-done(((f32[128,2048]{1,0:T(8,128)}), f32[128,2048]{1,0:T(8,128)}) %all-reduce.10.cloned.1.call-update) | async-done | bytes 1048592 | tf_op jit(solution)/shard_map/psum | solution.py:201
  535.6 4.7 fusion.73
  540.3 6.8 reduce-scatter.10.cloned.1.call-done
  550.7 17.4 %reduce-scatter.12.cloned.1.call-done = f32[128,128]{0,1:T(8,128)} async-done(((f32[512,128]{0,1:T(8,128)}), f32[128,128]{0,1:T(8,128)}) %reduce-scatter.12.cloned.1.call-update) | async-done | bytes 65552 | tf_op jit(solution)/shard_map/reduce_scatter | solution.py:267
  574.2 4.7 fusion.36
  584.5 10.5 fusion.74
  595.1 10.6 fusion.75
  606.8 10.4 fusion.42
  620.5 52.7 %all-reduce.2 = (f32[2048]{0:T(1024)S(1)}, f32[2048]{0:T(1024)S(1)}) all-reduce(f32[2048]{0:T(1024)S(1)} %get-tuple-element.97, f32[2048]{0:T(1024)S(1)} %get-tuple-element.95), channel_id=4, replica_groups=mesh['tensor'=2,'ctx'=4,'dp'=4] {'ctx','dp'}, use_global_device_ids=true, to_apply=%region_14.15.clone | all-reduce | flops 4096 | bytes 32768
  677.3 57.6 %reduce-scatter.18.cloned.1.call-done = f32[128,128]{1,0:T(8,128)} async-done(((f32[2048,128]{1,0:T(8,128)}), f32[128,128]{1,0:T(8,128)}) %reduce-scatter.18.cloned.1.call-update) | async-done | bytes 65552 | tf_op jit(solution)/shard_map/reduce_scatter | solution.py:298
  734.9 109.3 %reduce-scatter.14.cloned.1.call-done = f32[128,1024]{1,0:T(8,128)} async-done(((f32[2048,1024]{1,0:T(8,128)}), f32[128,1024]{1,0:T(8,128)}) %reduce-scatter.14.cloned.1.call-update) | async-done | bytes 524304 | tf_op jit(solution)/shard_map/reduce_scatter | solution.py:296
  844.2 109.7 %reduce-scatter.20.cloned.1.call-done = f32[1024,128]{1,0:T(8,128)} async-done(((f32[1024,2048]{1,0:T(8,128)}), f32[1024,128]{1,0:T(8,128)}) %reduce-scatter.20.cloned.1.call-update) | async-done | bytes 524304 | tf_op jit(solution)/shard_map/reduce_scatter | solution.py:299
  953.9 229.8 %reduce-scatter.22.cloned.1.call-done = f32[128,2816]{1,0:T(8,128)} async-done(((f32[2048,2816]{1,0:T(8,128)}), f32[128,2816]{1,0:T(8,128)}) %reduce-scatter.22.cloned.1.call-update) | async-done | bytes 1441808 | tf_op jit(solution)/shard_map/reduce_scatter | solution.py:301
  1183.7 231.1 %reduce-scatter.24.cloned.1.call-done = f32[128,2816]{1,0:T(8,128)} async-done(((f32[2048,2816]{1,0:T(8,128)}), f32[128,2816]{1,0:T(8,128)}) %reduce-scatter.24.cloned.1.call-update) | async-done | bytes 1441808 | tf_op jit(solution)/shard_map/reduce_scatter | solution.py:302
  1414.8 231.1 %reduce-scatter.26.cloned.1.call-done = f32[2816,128]{1,0:T(8,128)} async-done(((f32[2816,2048]{1,0:T(8,128)}), f32[2816,128]{1,0:T(8,128)}) %reduce-scatter.26.cloned.1.call-update) | async-done | bytes 1441808 | tf_op jit(solution)/shard_map/reduce_scatter | solution.py:303
  (156 shorter events, 67.5 us)
Async XLA Ops:
  7.2 82.4 %copy-start.2 = (bf16[1,128,2048]{2,1,0:T(8,128)(2,1)S(1)}, bf16[1,128,2048]{2,1,0:T(8,128)(2,1)}, u32[]{:S(2)}) copy-start(bf16[1,128,2048]{2,1,0:T(8,128)(2,1)} %param.12) | copy-start | bytes 1572868
  7.2 97.4 %all-gather.8.cloned.1.call-start = ((), (), s32[]{:S(2)}) async-start(), calls=%async_computation.9 | async-start | bytes 4456448 | tf_op jit(solution)/shard_map/all_gather | solution.py:83
  7.9 114.0 %all-gather.10.cloned.1.call-start = ((), (), s32[]{:S(2)}) async-start(), calls=%async_computation.10 | async-start | bytes 4456448 | tf_op jit(solution)/shard_map/all_gather | solution.py:86
  8.7 156.2 %all-reduce.8.cloned.1.call-start = ((), (), s32[]{:S(2)}) async-start(), calls=%async_computation.11 | async-start | bytes 2097152 | tf_op jit(solution)/shard_map/psum | solution.py:178
  29.4 81.7 %copy-start.22 = (f32[128]{0:T(128)}, f32[128]{0:T(128)S(1)}, u32[]{:S(2)}) copy-start(f32[128]{0:T(128)S(1)} %get-tuple-element.142) | copy-start | bytes 1540
  65.9 51.2 %copy-start.20 = (bf16[512,128]{0,1:T(8,128)(2,1)}, bf16[512,128]{0,1:T(8,128)(2,1)S(1)}, u32[]{:S(2)}) copy-start(bf16[512,128]{0,1:T(8,128)(2,1)S(1)} %copy.41) | copy-start | bytes 393220
  89.2 22.0 %copy-start.4 = (bf16[2048,128]{1,0:T(8,128)(2,1)}, bf16[2048,128]{1,0:T(8,128)(2,1)S(1)}, u32[]{:S(2)}) copy-start(bf16[2048,128]{1,0:T(8,128)(2,1)S(1)} %all_gather.36) | copy-start | bytes 1572868
  104.4 10.3 copy-start.17
  125.9 134.6 %all-gather.12.cloned.1.call-start = ((), (), s32[]{:S(2)}) async-start(), calls=%async_computation.12 | async-start | bytes 12255232 | tf_op jit(solution)/shard_map/all_gather | solution.py:88
  126.4 228.9 %all-gather.14.cloned.1.call-start = ((), (), s32[]{:S(2)}) async-start(), calls=%async_computation.13 | async-start | bytes 12255232 | tf_op jit(solution)/shard_map/all_gather | solution.py:89
  127.0 325.4 %all-gather.16.cloned.1.call-start = ((), (), s32[]{:S(2)}) async-start(), calls=%async_computation.14 | async-start | bytes 12255232 | tf_op jit(solution)/shard_map/all_gather | solution.py:90
  127.6 388.2 %all-reduce.10.cloned.1.call-start = ((), (), s32[]{:S(2)}) async-start(), calls=%async_computation.15 | async-start | bytes 2097152 | tf_op jit(solution)/shard_map/psum | solution.py:201
  144.1 373.4 %copy-start.24 = (pred[128]{0:T(512)(128)(4,1)}, pred[128]{0:T(512)(128)(4,1)S(1)}, u32[]{:S(2)}) copy-start(pred[128]{0:T(512)(128)(4,1)S(1)} %broadcast_compare_fusion) | copy-start | bytes 388
  267.5 185.0 %copy-start.9 = (bf16[1,128,2048]{2,1,0:T(8,128)(2,1)S(1)}, bf16[1,128,2048]{2,1,0:T(8,128)(2,1)}, u32[]{:S(2)}) copy-start(bf16[1,128,2048]{2,1,0:T(8,128)(2,1)} %param.23) | copy-start | bytes 1572868
  452.5 18.3 %slice-start = ((s8[11534336]{0:T(1024)(128)(4,1)}), s8[4194304]{0:T(1024)(128)(4,1)S(1)}, s32[]{:S(2)}) async-start(s8[11534336]{0:T(1024)(128)(4,1)} %bitcast.165), calls=%async_computation.26 | async-start | bytes 8388608
  452.5 18.3 %slice-start.1 = ((s8[11534336]{0:T(1024)(128)(4,1)}), s8[3145728]{0:T(1024)(128)(4,1)S(1)}, s32[]{:S(2)}) async-start(s8[11534336]{0:T(1024)(128)(4,1)} %bitcast.165), calls=%async_computation.27 | async-start | bytes 6291456
  461.8 8.9 copy-start.7
  461.9 8.9 copy-start.6
  461.9 14.0 copy-start.5
  461.9 8.9 slice-start.2
  475.6 71.6 %reduce-scatter.10.cloned.1.call-start = ((), (), s32[]{:S(2)}) async-start(), calls=%async_computation.16 | async-start | bytes 327680 | tf_op jit(solution)/shard_map/reduce_scatter | solution.py:266
  530.3 37.7 %reduce-scatter.12.cloned.1.call-start = ((), (), s32[]{:S(2)}) async-start(), calls=%async_computation.17 | async-start | bytes 327680 | tf_op jit(solution)/shard_map/reduce_scatter | solution.py:267
  535.5 83.6 %all-reduce.12.cloned.1.call-start = ((), (), s32[]{:S(2)}) async-start(), calls=%async_computation.25 | async-start | bytes 2097152 | tf_op jit(solution)/shard_map/psum | solution.py:187
  548.0 24.8 %copy-start.23 = (f32[128]{0:T(128)S(1)}, f32[128]{0:T(128)}, u32[]{:S(2)}) copy-start(f32[128]{0:T(128)} %copy-done.22) | copy-start | bytes 1540
  570.6 106.7 %reduce-scatter.16.cloned.1.call-start = ((), (), s32[]{:S(2)}) async-start(), calls=%async_computation.19 | async-start | bytes 1114112 | tf_op jit(solution)/shard_map/reduce_scatter | solution.py:297
  572.7 162.2 %reduce-scatter.18.cloned.1.call-start = ((), (), s32[]{:S(2)}) async-start(), calls=%async_computation.20 | async-start | bytes 1114112 | tf_op jit(solution)/shard_map/reduce_scatter | solution.py:298
  574.2 270.0 %reduce-scatter.14.cloned.1.call-start = ((), (), s32[]{:S(2)}) async-start(), calls=%async_computation.18 | async-start | bytes 8912896 | tf_op jit(solution)/shard_map/reduce_scatter | solution.py:296
  578.9 374.9 %reduce-scatter.20.cloned.1.call-start = ((), (), s32[]{:S(2)}) async-start(), calls=%async_computation.21 | async-start | bytes 8912896 | tf_op jit(solution)/shard_map/reduce_scatter | solution.py:299
  584.5 599.2 %reduce-scatter.22.cloned.1.call-start = ((), (), s32[]{:S(2)}) async-start(), calls=%async_computation.22 | async-start | bytes 24510464 | tf_op jit(solution)/shard_map/reduce_scatter | solution.py:301
  595.1 819.7 %reduce-scatter.24.cloned.1.call-start = ((), (), s32[]{:S(2)}) async-start(), calls=%async_computation.23 | async-start | bytes 24510464 | tf_op jit(solution)/shard_map/reduce_scatter | solution.py:302
  605.8 1040.1 %reduce-scatter.26.cloned.1.call-start = ((), (), s32[]{:S(2)}) async-start(), calls=%async_computation.24 | async-start | bytes 24510464 | tf_op jit(solution)/shard_map/reduce_scatter | solution.py:303
  617.2 57.2 %copy-start.26 = (f32[128]{0:T(128)S(1)}, f32[128]{0:T(128)}, u32[]{:S(2)}) copy-start(f32[128]{0:T(128)} %get-tuple-element.141) | copy-start | bytes 1540
  (17 other events, 44.5 us)
Sparse Core Ops, SparseCore 0:
  10.2 55.2 all-gather.7
  67.6 54.2 all-gather.9
  126.0 38.8 all-reduce.7
  167.2 93.1 all-gather.11
  262.8 92.4 all-gather.13
  357.6 94.8 all-gather.15
  475.7 40.0 all-reduce.9
  530.4 16.6 reduce-scatter.9
  550.1 17.9 reduce-scatter.11
  570.8 41.4 all-reduce.11
  616.9 57.4 reduce-scatter.15
  678.5 56.3 reduce-scatter.17
  740.1 104.0 reduce-scatter.13
  849.2 104.5 reduce-scatter.19
  959.0 224.7 reduce-scatter.21
  1188.8 225.9 reduce-scatter.23
  1419.9 225.9 reduce-scatter.25
where the time goes:
time: 1660 us; the launch traced here: 1650 us
  waiting for transfers between devices  1320 us (80%)
  blocking collectives  159 us (10%)
  matrix products  122 us (7%)
    reduce_scatter x1, waiting for transfers between devices, shards(): lax.psum_scatter(grad_up, ('ctx', 'dp'), scatter_dimension=0, tiled=True)  231 us
    reduce_scatter x1, waiting for transfers between devices, shards(): lax.psum_scatter(grad_down, ('ctx', 'dp'), scatter_dimension=1, tiled=True)  231 us
    reduce_scatter x1, waiting for transfers between devices, shards(): lax.psum_scatter(grad_gate, ('ctx', 'dp'), scatter_dimension=0, tiled=True)  230 us
    reduce_scatter x1, waiting for transfers between devices, shards(): lax.psum_scatter(grad_out, ('ctx', 'dp'), scatter_dimension=1, tiled=True)  110 us
    reduce_scatter x1, waiting for transfers between devices, shards(): lax.psum_scatter(grad_query, ('ctx', 'dp'), scatter_dimension=0, tiled=True)  109 us
    all_gather x1, waiting for transfers between devices, shards(): lax.all_gather(w_gate, ('ctx', 'dp'), axis=0, tiled=True)  94 us
    all_gather x1, waiting for transfers between devices, shards(): lax.all_gather(w_down, ('ctx', 'dp'), axis=1, tiled=True)  90.1 us
    all_gather x1, waiting for transfers between devices, shards(): lax.all_gather(w_up, ('ctx', 'dp'), axis=0, tiled=True)  87.9 us
  transfers between devices with their start and end apart: 17, of which 14 were waited for; matrix products, arithmetic and copies ran while one was open for 6% of the time, Pallas kernels for 0%

commit v1 on v0

--- a/solution.py
+++ b/solution.py
@@ -1,6 +1,10 @@
+import functools
+
 import jax
 import jax.numpy as jnp
 from jax import lax
+from jax.experimental import pallas as pl
+from jax.experimental.pallas import tpu as pltpu
 from jax.sharding import PartitionSpec as P
 
 HEAD_SIZE = 64
@@ -318,6 +322,1295 @@
     )
 
 
+MESH = pl.DeviceIdType.MESH
+HBM = pltpu.MemorySpace.HBM
+VMEM = pltpu.MemorySpace.VMEM
+STEPS = [(1, -1), (1, 1), (2, -1), (2, 1), (3, -1), (3, 1)]
+
+
+def position():
+    t, c, d = lax.axis_index("tensor"), lax.axis_index("ctx"), lax.axis_index("dp")
+    return t, c, d // 2, d % 2
+
+
+def only(cond, act):
+    if cond is True:
+        act()
+    else:
+        pl.when(cond)(act)
+
+
+class Wires:
+    def __init__(self, send, recv):
+        self.send, self.recv, self.used, self.sent = send, recv, 0, []
+
+    def index(self):
+        self.used += 1
+        return self.used - 1
+
+    def copy(self, i, src, dst, device, lands=None):
+        return pltpu.make_async_remote_copy(
+            src_ref=src,
+            dst_ref=dst,
+            send_sem=self.send.at[i],
+            recv_sem=self.recv.at[i if lands is None else lands],
+            device_id=device,
+            device_id_type=MESH,
+        )
+
+    def push(self, i, src, dst, device, cond=True, lands=None):
+        only(cond, lambda: self.copy(i, src(), dst(), device, lands).start())
+        self.sent.append((cond, lambda: self.copy(i, src(), dst(), device).wait_send()))
+
+    def owe(self, i, src, cond=True):
+        self.sent.append((cond, lambda: self.copy(i, src(), src(), position_id()).wait_send()))
+
+    def arrive(self, i, dst, cond=True):
+        def act():
+            place = dst()
+            self.copy(i, place, place, position_id()).wait_recv()
+
+        only(cond, act)
+
+    def local(self, i, src, dst):
+        def make():
+            return pltpu.make_async_copy(src(), dst(), self.send.at[i])
+
+        make().start()
+        self.sent.append((True, lambda: make().wait()))
+
+    def fetch(self, i, src, dst):
+        copy = pltpu.make_async_copy(src, dst, self.recv.at[i])
+        copy.start()
+        return copy
+
+    def drain(self):
+        for cond, act in self.sent:
+            only(cond, act)
+        self.sent = []
+
+
+def position_id():
+    t, c, y, e = position()
+    return (t, c, y * 2 + e)
+
+
+def greet(peers):
+    barrier = pltpu.get_barrier_semaphore()
+    count = 0
+    for cond, device in peers:
+        only(
+            cond,
+            functools.partial(
+                pl.semaphore_signal, barrier, inc=1, device_id=device, device_id_type=MESH
+            ),
+        )
+        count = count + (1 if cond is True else cond.astype(jnp.int32))
+    pl.semaphore_wait(barrier, count)
+
+
+def around(pos, chain=True, x=False, y=False, core=True, row=False):
+    t, c, yy, e = pos
+    d = yy * 2 + e
+    peers = []
+    if chain:
+        peers += [(c < 3, (t, c + 1, d)), (c > 0, (t, c - 1, d))]
+    if x:
+        peers.append((True, (1 - t, c, d)))
+    if y:
+        peers.append((True, (t, c, (1 - yy) * 2 + e)))
+    if core:
+        peers.append((True, (t, c, yy * 2 + 1 - e)))
+    return peers
+
+
+def reach(c, s, sign):
+    k = c + sign * s
+    return k, ((k >= 0) if sign < 0 else (k <= 3))
+
+
+def plane_gather(wires, pos, src, at):
+    t, c, y, e = pos
+    d, d_y, d_e = y * 2 + e, (1 - y) * 2 + e, y * 2 + 1 - e
+    z_id = {key: wires.index() for key in STEPS}
+    y_id = {key: wires.index() for key in [(0, 0)] + STEPS}
+    e_id = {key: wires.index() for key in [(0, 0)] + STEPS}
+    f_id = {key: wires.index() for key in [(0, 0)] + STEPS}
+    fetch = wires.fetch(wires.index(), src(), at(c, d))
+
+    def spread(key, block, place, cond):
+        s, sign = key
+        if s < 3:
+            for way in ((-1, 1) if s == 0 else (sign,)):
+                nxt = c - way
+                here = (nxt >= 0) if way > 0 else (nxt <= 3)
+                wires.push(
+                    z_id[(s + 1, way)], block, place, (t, nxt, d),
+                    here if cond is True else (cond & here),
+                )
+        wires.push(y_id[key], block, place, (t, c, d_y), cond)
+        wires.push(e_id[key], block, place, (t, c, d_e), cond)
+
+    def relay(key, cond):
+        k = c + key[0] * key[1]
+        place = lambda: at(k, d_y)
+        wires.arrive(y_id[key], place, cond)
+        wires.push(f_id[key], place, place, (t, c, d_e), cond)
+
+    spread((0, 0), src, lambda: at(c, d), True)
+    yield
+    late = [((0, 0), True)]
+    for key in STEPS:
+        k, cond = reach(c, *key)
+        place = lambda k=k: at(k, d)
+        wires.arrive(z_id[key], place, cond)
+        spread(key, place, place, cond)
+        if key[1] > 0:
+            for old in late:
+                relay(*old)
+            late = []
+            yield
+        late.append((key, cond))
+    for old in late:
+        relay(*old)
+    yield
+    for key in [(0, 0)] + STEPS:
+        k, cond = (c, True) if key[0] == 0 else reach(c, *key)
+        wires.arrive(e_id[key], lambda: at(k, d_e), cond)
+        wires.arrive(f_id[key], lambda: at(k, (1 - y) * 2 + 1 - e), cond)
+    fetch.wait()
+
+
+def token_gather(wires, pos, src, at, half):
+    t, c, y, e = pos
+    d, d_e = y * 2 + e, y * 2 + 1 - e
+    z_id = {key: wires.index() for key in STEPS}
+    x_id = {key: wires.index() for key in STEPS}
+    e_id = {key: wires.index() for key in STEPS}
+    f_id = {key: wires.index() for key in STEPS}
+    own = wires.index(), wires.index()
+    here = wires.index(), wires.index()
+    for way in (-1, 1):
+        nxt = c - way
+        wires.push(
+            z_id[(1, way)], lambda: half(t), lambda: at(e, c, t), (t, nxt, d),
+            (nxt >= 0) if way > 0 else (nxt <= 3),
+        )
+    for i in (0, 1):
+        wires.push(own[i], lambda i=i: half(i), lambda i=i: at(e, c, i), (t, c, d_e))
+    fetch = [wires.fetch(here[i], half(i), at(e, c, i)) for i in (0, 1)]
+    yield
+
+    def relay(key, cond):
+        k = c + key[0] * key[1]
+        place = lambda: at(e, k, 1 - t)
+        wires.arrive(x_id[key], place, cond)
+        wires.push(f_id[key], place, place, (t, c, d_e), cond)
+
+    late = []
+    for key in STEPS:
+        k, cond = reach(c, *key)
+        place = lambda k=k: at(e, k, t)
+        wires.arrive(z_id[key], place, cond)
+        s, sign = key
+        if s < 3:
+            nxt = c - sign
+            ok = (nxt >= 0) if sign > 0 else (nxt <= 3)
+            wires.push(z_id[(s + 1, sign)], place, place, (t, nxt, d), cond & ok)
+        wires.push(x_id[key], place, place, (1 - t, c, d), cond)
+        wires.push(e_id[key], place, place, (t, c, d_e), cond)
+        if sign > 0:
+            for old in late:
+                relay(*old)
+            late = []
+            yield
+        late.append((key, cond))
+    for old in late:
+        relay(*old)
+    yield
+    for i in (0, 1):
+        wires.arrive(own[i], lambda i=i: at(1 - e, c, i))
+    for key in STEPS:
+        k, cond = reach(c, *key)
+        wires.arrive(e_id[key], lambda: at(1 - e, k, t), cond)
+        wires.arrive(f_id[key], lambda: at(1 - e, k, 1 - t), cond)
+    for copy in fetch:
+        copy.wait()
+
+
+def unit_scatter(wires, pos, piece, place):
+    t, c, y, e = pos
+    me = c * 2 + e
+    first = [wires.index() for _ in range(8)]
+    second = [wires.index() for _ in range(8)]
+    fetch = wires.fetch(first[0], piece(me), place(c, y * 2 + e))
+    for i in range(1, 8):
+        q = lax.rem(me + i, 8)
+        wires.push(
+            first[i], lambda q=q: piece(q), lambda: place(c, y * 2 + e), (t, q // 2, y * 2 + q % 2)
+        )
+    wires.push(
+        second[0], lambda: piece(me), lambda: place(c, y * 2 + e), (t, c, (1 - y) * 2 + e)
+    )
+    yield
+    for i in range(1, 8):
+        q = lax.rem(me + 8 - i, 8)
+        block = lambda q=q: place(q // 2, y * 2 + q % 2)
+        wires.arrive(first[i], block)
+        wires.push(second[i], block, block, (t, c, (1 - y) * 2 + e))
+        yield
+    yield
+    for i in range(8):
+        q = lax.rem(me + 8 - i, 8)
+        wires.arrive(second[i], lambda q=q: place(q // 2, (1 - y) * 2 + q % 2))
+    fetch.wait()
+
+
+def run_all(parts):
+    parts = list(parts)
+    while parts:
+        for part in list(parts):
+            try:
+                next(part)
+            except StopIteration:
+                parts.remove(part)
+
+
+def rows(ref, start, size):
+    return ref.at[pl.ds(pl.multiple_of(start, 16), size)]
+
+
+def dot_nn(a, b):
+    return lax.dot_general(a, b, (((1,), (0,)), ((), ())), preferred_element_type=jnp.float32)
+
+
+def by_rows(count, step, act):
+    def body(i, carry):
+        act(pl.ds(pl.multiple_of(i * step, step), step))
+        return carry
+
+    lax.fori_loop(0, count // step, body, 0)
+
+
+ORDER = (3, 0, 2, 1)
+
+
+def chain_sum(wires, pos, height, value, keep, came, extra, done):
+    t, c, y, e = pos
+    d = y * 2 + e
+    wide = jnp.float32
+    r_id = [wires.index() for _ in range(4)]
+    l_id = [wires.index() for _ in range(4)]
+
+    def hop(k):
+        place = keep(k)
+        for go, edge, number, way in ((c < k, 0, r_id[k], 1), (c > k, 3, l_id[k], -1)):
+            if (k == 0 and way > 0) or (k == 3 and way < 0):
+                continue
+            wires.arrive(number, lambda: came.at[k], go & (c != edge))
+
+            def act():
+                def first(r):
+                    place[r] = value(k, r).astype(place.dtype)
+
+                def later(r):
+                    place[r] = (value(k, r) + came[k, r].astype(wide)).astype(place.dtype)
+
+                pl.when(c == edge)(lambda: by_rows(height, 16, first))
+                pl.when(c != edge)(lambda: by_rows(height, 16, later))
+
+            pl.when(go)(act)
+            target = (t, c + way, d)
+            if way > 0:
+                wires.push(number, lambda: keep(k), lambda: came.at[k], target, go)
+            else:
+                wires.push(number, lambda: keep(k), lambda: extra, target, go & (c == k + 1))
+                wires.push(number, lambda: keep(k), lambda: came.at[k], target, go & (c > k + 1))
+
+    def finish():
+        for k in range(4):
+
+            def act(k=k):
+                if k > 0:
+                    wires.arrive(r_id[k], lambda: came.at[k])
+                if k < 3:
+                    wires.arrive(l_id[k], lambda: extra)
+
+                def add(r):
+                    total = value(k, r)
+                    if k > 0:
+                        total = total + came[k, r].astype(wide)
+                    if k < 3:
+                        total = total + extra[r].astype(wide)
+                    done(r, total)
+
+                by_rows(height, 16, add)
+
+            pl.when(c == k)(act)
+
+    return hop, finish
+
+
+def token_scatter(wires, pos, part, out, scratch):
+    t, c, y, e = pos
+    near, own, x_in, came, extra = scratch
+    wide = jnp.float32
+    tokens, half = x_in.shape[1], x_in.shape[2]
+    d_e = y * 2 + 1 - e
+    e_id = [wires.index() for _ in range(4)]
+    x_id = [wires.index() for _ in range(4)]
+    last = wires.index()
+    mine = pl.ds(pl.multiple_of(t * half, 128), half)
+    other = pl.ds(pl.multiple_of((1 - t) * half, 128), half)
+
+    def begin(k, f):
+        return pl.multiple_of((k * 2 + f) * tokens, 16)
+
+    for k in ORDER:
+        wires.push(
+            e_id[k], lambda k=k: part.at[pl.ds(begin(k, 1 - e), tokens)],
+            lambda k=k: near.at[k], (t, c, d_e),
+        )
+    fetch = [
+        wires.fetch(wires.index(), part.at[pl.ds(begin(k, e), tokens)], own.at[k]) for k in range(4)
+    ]
+    yield
+    for k in ORDER:
+        fetch[k].wait()
+        wires.arrive(e_id[k], lambda: near.at[k])
+
+        def away(r):
+            total = own[k, r, other].astype(wide) + near[k, r, other].astype(wide)
+            near[k, r, other] = total.astype(near.dtype)
+
+        by_rows(tokens, 16, away)
+        wires.push(
+            x_id[k], lambda k=k: near.at[k, :, other], lambda k=k: x_in.at[k], (1 - t, c, y * 2 + e)
+        )
+    yield
+
+    def value(k, r):
+        return (
+            own[k, r, mine].astype(wide)
+            + near[k, r, mine].astype(wide)
+            + x_in[k, r].astype(wide)
+        )
+
+    def done(r, total):
+        out[r, mine] = total.astype(out.dtype)
+
+    hop, finish = chain_sum(
+        wires, pos, tokens, value, lambda k: near.at[k, :, mine], came, extra, done
+    )
+    for k in ORDER:
+        wires.arrive(x_id[k], lambda: x_in.at[k])
+        hop(k)
+        yield
+    finish()
+    wires.push(last, lambda: out.at[:, mine], lambda: out.at[:, mine], (1 - t, c, y * 2 + e))
+    yield
+    wires.arrive(last, lambda: out.at[:, other])
+
+
+def token_scratch(tokens, width):
+    low, half = jnp.bfloat16, width // 2
+    return [
+        pltpu.VMEM((4, tokens, width), low),
+        pltpu.VMEM((4, tokens, width), low),
+        pltpu.VMEM((4, tokens, half), low),
+        pltpu.VMEM((4, tokens, half), low),
+        pltpu.VMEM((tokens, half), low),
+    ]
+
+
+def plane_scatter(wires, pos, out_block, own_block, height, scratch, done):
+    t, c, y, e = pos
+    near, y_in, came, extra = scratch
+    wide = jnp.float32
+    d_y, d_e = (1 - y) * 2 + e, y * 2 + 1 - e
+    e_id = {(k, f): wires.index() for k in range(4) for f in range(2)}
+    y_id = [wires.index() for _ in range(4)]
+    for f in range(2):
+        yy = (1 - y) if f == 0 else y
+        for k in ORDER:
+            wires.push(
+                e_id[k, f], lambda k=k, yy=yy: out_block(k, yy),
+                lambda k=k, f=f: near.at[f * 4 + k], (t, c, d_e),
+            )
+    yield
+    for k in ORDER:
+        wires.arrive(e_id[k, 0], lambda: near.at[k])
+        block = own_block(k, 1 - y)
+
+        def away(r):
+            total = block[r].astype(wide) + near[k, r].astype(wide)
+            near[k, r] = total.astype(near.dtype)
+
+        by_rows(height, 16, away)
+        wires.push(y_id[k], lambda k=k: near.at[k], lambda k=k: y_in.at[k], (t, c, d_y))
+        yield
+
+    def value(k, r):
+        return (
+            own_block(k, y)[r].astype(wide)
+            + near[4 + k, r].astype(wide)
+            + y_in[k, r].astype(wide)
+        )
+
+    hop, finish = chain_sum(
+        wires, pos, height, value, lambda k: near.at[4 + k], came, extra, done
+    )
+    for k in ORDER:
+        wires.arrive(e_id[k, 1], lambda: near.at[4 + k])
+        wires.arrive(y_id[k], lambda: y_in.at[k])
+        hop(k)
+        yield
+    finish()
+
+
+def plane_scratch(shape):
+    low = jnp.bfloat16
+    return [
+        pltpu.VMEM((8,) + shape, low),
+        pltpu.VMEM((4,) + shape, low),
+        pltpu.VMEM((4,) + shape, low),
+        pltpu.VMEM(shape, low),
+    ]
+
+
+def unit_gather(wires, pos, sums, out):
+    t, c, y, e = pos
+    units, lanes = sums.shape[2], out.shape[2]
+    me = c * 2 + e
+    o_id = [wires.index() for _ in range(8)]
+    here = pl.ds(pl.multiple_of(me * units, 16), units)
+    for i in range(1, 8):
+        q = lax.rem(me + i, 8)
+        wires.push(
+            o_id[i],
+            lambda q=q: sums.at[q // 2, :, :, pl.ds(pl.multiple_of((q % 2) * lanes, 128), lanes)],
+            lambda: out.at[:, here], (t, q // 2, y * 2 + q % 2),
+        )
+    fetch = wires.fetch(
+        wires.index(), sums.at[c, :, :, pl.ds(pl.multiple_of(e * lanes, 128), lanes)], out.at[:, here]
+    )
+    yield
+    for i in range(1, 8):
+        q = lax.rem(me + 8 - i, 8)
+        wires.arrive(o_id[i], lambda: out.at[:, pl.ds(pl.multiple_of(q * units, 16), units)])
+    fetch.wait()
+
+
+def swap_halves(x):
+    lane = lax.broadcasted_iota(jnp.int32, x.shape, 1)
+    ahead, behind = pltpu.roll(x, x.shape[1] - 32, 1), pltpu.roll(x, 32, 1)
+    return jnp.where(lax.rem(lane, 64) < 32, ahead, behind)
+
+
+def head_probs(query, keys, allowed):
+    scores = times_transposed(query, keys) * (HEAD_SIZE ** (-0.5))
+    scores = jnp.where(allowed, scores, NEGATIVE)
+    shifted = jnp.exp(scores - jnp.max(scores, axis=-1, keepdims=True))
+    return shifted * (1.0 / jnp.sum(shifted, axis=-1, keepdims=True))
+
+
+def norm_rows(upstream, inputs, gain):
+    rms = lax.rsqrt(jnp.mean(inputs * inputs, axis=-1, keepdims=True) + EPS)
+    gain_grad = jnp.sum(upstream * inputs * rms, axis=0, keepdims=True)
+    scaled = upstream * gain
+    inner = jnp.mean(scaled * inputs, axis=-1, keepdims=True)
+    return rms * scaled - inputs * (rms * rms * rms * inner), gain_grad
+
+
+def advance(parts, count=1):
+    for _ in range(count):
+        for part in list(parts):
+            try:
+                next(part)
+            except StopIteration:
+                parts.remove(part)
+
+
+def backward_kernel(
+    lengths, gn, part_b, g3, qkv_hbm, out_hbm, gain_all, hidden, states, gy, normed_one, q_rot, kv_all,
+    mixed, cosine, sine,
+    layer_out, grad_states, g3_out, gq_out, go_out, gain_out,
+    send, recv, grad_low, branch, grad_hidden, mixed_t, go_part, grad_mixed, gqkv, normed_t, gq_part,
+    dk, dv, kv_part, kv_in, pair_out, pair_in, gains, gain_in, qkv_all, out_all, *scratch,
+):
+    pos = position()
+    t, c, y, e = pos
+    low, wide = jnp.bfloat16, jnp.float32
+    wires = Wires(send, recv)
+    d = y * 2 + e
+    me = c * 4 + d
+    peers = [(True, (1 - t, c, d))]
+    for i in range(1, 16):
+        q = lax.rem(me + i, 16)
+        peers.append((True, (t, q // 4, lax.rem(q, 4))))
+    greet(peers)
+    tokens, width = states.shape
+    n_query = q_rot.shape[1]
+    n_key = kv_all.shape[1] // 2
+    lanes = go_out.shape[1]
+    rows_out = go_out.shape[0]
+    t_b, s_q, s_k, s_o = scratch[:5], scratch[5:9], scratch[9:13], scratch[13:17]
+    load_out = wires.fetch(wires.index(), out_hbm, out_all)
+    load_qkv = wires.fetch(wires.index(), qkv_hbm, qkv_all)
+
+    units = [unit_gather(wires, pos, g3, g3_out)]
+    second = [token_scatter(wires, pos, part_b, branch, t_b)]
+    advance(units)
+    mixed_t[...] = mixed[...].T
+    normed_t[...] = normed_one[...].T
+    advance(second)
+
+    gains[...] = jnp.zeros_like(gains)
+    gain_one = gain_all[...].astype(wide)[0:1]
+    gain_two = gain_all[...].astype(wide)[1:2]
+
+    def norm_two(r):
+        value, grad = norm_rows(gn[r].astype(wide), hidden[r], gain_two)
+        total = gy[r].astype(wide) + value
+        grad_hidden[r] = total
+        grad_low[r] = total.astype(low)
+        gains[1:2] += grad
+
+    by_rows(tokens, 16, norm_two)
+
+    def out_grad(j, carry):
+        where = pl.ds(pl.multiple_of(j * 2 * lanes, 256), 2 * lanes)
+        go_part[j] = dot_nn(mixed_t[...], grad_low[:, where]).astype(low)
+        return carry
+
+    lax.fori_loop(0, 8, out_grad, 0)
+    outs = [
+        plane_scatter(
+            wires, pos,
+            lambda k, yy: go_part.at[k * 2 + yy, :, pl.ds(pl.multiple_of((1 - e) * lanes, 128), lanes)],
+            lambda k, yy: go_part.at[k * 2 + yy, :, pl.ds(pl.multiple_of(e * lanes, 128), lanes)],
+            rows_out, s_o, lambda r, v: go_out.__setitem__(r, v),
+        )
+    ]
+    advance(outs)
+
+    load_out.wait()
+
+    def mix_grad(j, carry):
+        where = pl.ds(pl.multiple_of(j * 256, 256), 256)
+        grad_mixed[:, where] = times_transposed(grad_low[...], out_all[where, :]).astype(low)
+        return carry
+
+    lax.fori_loop(0, n_query // 256, mix_grad, 0)
+
+    q_pos = c * tokens + lax.broadcasted_iota(jnp.int32, (tokens, kv_all.shape[0]), 0)
+    k_pos = lax.broadcasted_iota(jnp.int32, (tokens, kv_all.shape[0]), 1)
+    allowed = (k_pos <= q_pos) & (k_pos < lengths[0])
+    scale = HEAD_SIZE ** (-0.5)
+    pairs = n_query // 256
+    for g in range(2):
+        keys = kv_all[:, g * HEAD_SIZE : (g + 1) * HEAD_SIZE]
+        values = kv_all[:, n_key + g * HEAD_SIZE : n_key + (g + 1) * HEAD_SIZE]
+        dk[...] = jnp.zeros_like(dk)
+        dv[...] = jnp.zeros_like(dv)
+
+        def pair(j, carry, g=g, keys=keys, values=values):
+            slab = pl.ds(pl.multiple_of((g * pairs + j) * 128, 128), 128)
+            q_two, m_two = q_rot[:, slab], grad_mixed[:, slab]
+            both = []
+            for h in range(2):
+                query = q_two[:, h * HEAD_SIZE : (h + 1) * HEAD_SIZE]
+                upstream = m_two[:, h * HEAD_SIZE : (h + 1) * HEAD_SIZE]
+                probs = head_probs(query, keys, allowed)
+                dprob = times_transposed(upstream, values)
+                delta = jnp.sum(probs * dprob, axis=-1, keepdims=True)
+                grad_scores = (probs * (dprob - delta)).astype(low)
+                both.append(dot_nn(grad_scores, keys))
+                dk[...] += transposed_times(grad_scores, query)
+                dv[...] += transposed_times(probs.astype(low), upstream)
+            grads = jnp.concatenate(both, axis=1) * scale
+            back = grads * cosine[...] - swap_halves(grads) * sine[...]
+            gqkv[:, slab] = back.astype(low)
+            return carry
+
+        lax.fori_loop(0, pairs, pair, 0)
+        for k in range(4):
+            block = slice(k * tokens, (k + 1) * tokens)
+            kv_part[k, :, g * HEAD_SIZE : (g + 1) * HEAD_SIZE] = (dk[block] * scale).astype(low)
+            kv_part[k, :, n_key + g * HEAD_SIZE : n_key + (g + 1) * HEAD_SIZE] = dv[block].astype(low)
+        advance(outs)
+
+    kv_id = [wires.index() for _ in range(3)]
+    for i in range(3):
+        k = lax.rem(c + i + 1, 4)
+        wires.push(kv_id[i], lambda k=k: kv_part.at[k], lambda i=i: kv_in.at[i], (t, k, d))
+
+    def q_grad(core, where):
+        def act(j, carry):
+            owner = j * 2 + core
+            here = pl.ds(pl.multiple_of(owner * lanes, 128), lanes)
+            gq_part[owner, :, where] = dot_nn(normed_t[here, :], gqkv[:, where]).astype(low)
+            return carry
+
+        lax.fori_loop(0, 8, act, 0)
+
+    def q_sums(where, scratches):
+        def done(r, value):
+            gq_out[r, where] = value
+
+        return plane_scatter(
+            wires, pos,
+            lambda k, yy: gq_part.at[k * 4 + yy * 2 + 1 - e, :, where],
+            lambda k, yy: gq_part.at[k * 4 + yy * 2 + e, :, where],
+            gq_out.shape[0], scratches, done,
+        )
+
+    first, rest = slice(0, n_query), slice(n_query, n_query + 2 * n_key)
+    q_grad(1 - e, first)
+    queries = [q_sums(first, s_q)]
+    advance(queries)
+    q_grad(e, first)
+    for _ in range(4):
+        advance(queries)
+    total = kv_part[c].astype(wide)
+    for i in range(3):
+        wires.arrive(kv_id[i], lambda: kv_in.at[i])
+        total = total + kv_in[i].astype(wide)
+    key_grads = total[:, :n_key]
+    key_grads = key_grads * cosine[...] - swap_halves(key_grads) * sine[...]
+    gqkv[:, n_query : n_query + n_key] = key_grads.astype(low)
+    gqkv[:, n_query + n_key :] = total[:, n_key:].astype(low)
+    q_grad(1 - e, rest)
+    others = [q_sums(rest, s_k)]
+    advance(others)
+    q_grad(e, rest)
+    load_qkv.wait()
+
+    def normed_grad(j, carry):
+        where = pl.ds(pl.multiple_of(j * 256, 256), 256)
+        pair_out[:, where] = times_transposed(gqkv[...], qkv_all[where, :]).astype(low)
+        return carry
+
+    lax.fori_loop(0, width // 256, normed_grad, 0)
+    p_id = wires.index()
+    wires.push(p_id, lambda: pair_out, lambda: pair_in, (1 - t, c, d))
+    for _ in range(4):
+        advance(others)
+    advance(second)
+    wires.arrive(p_id, lambda: pair_in)
+
+    def norm_one(r):
+        upstream = pair_out[r].astype(wide) + pair_in[r].astype(wide)
+        value, grad = norm_rows(upstream, states[r].astype(wide), gain_one)
+        grad_states[r] = grad_hidden[r] + value
+        gains[0:1] += grad
+
+    by_rows(tokens, 16, norm_one)
+    g_id = [wires.index() for _ in range(16)]
+
+    def gain_block(q):
+        return gains.at[:, pl.ds(pl.multiple_of(q * lanes, 128), lanes)]
+
+    for i in range(1, 16):
+        q = lax.rem(me + i, 16)
+        wires.push(
+            g_id[i], lambda q=q: gain_block(q), lambda i=i: gain_in.at[i],
+            (t, q // 4, lax.rem(q, 4)),
+        )
+    while second or outs or queries or others:
+        advance(outs)
+        advance(queries)
+        advance(others)
+        advance(second)
+    advance(units)
+
+    def finish(r):
+        layer_out[r] = (hidden[r] + branch[r].astype(wide)).astype(low)
+
+    by_rows(tokens, 16, finish)
+    gain = gains[:, pl.ds(pl.multiple_of(me * lanes, 128), lanes)]
+    for i in range(1, 16):
+        wires.arrive(g_id[i], lambda: gain_in.at[i])
+        gain = gain + gain_in[i]
+    gain_out[...] = gain
+    wires.drain()
+
+
+def backward_call(
+    lengths, gn, part_b, g3, qkv_all, out_all, gain_all, hidden, states, gy, normed_one, q_rot, kv_all,
+    mixed, cosine, sine,
+):
+    shape = jax.ShapeDtypeStruct
+    low, wide = jnp.bfloat16, jnp.float32
+    units = g3.shape[2]
+    tokens, width = states.shape
+    n_query, keys = q_rot.shape[1], kv_all.shape[0]
+    n_all = qkv_all.shape[1]
+    lanes = width // 16
+    vm = pltpu.VMEM
+    return pl.pallas_call(
+        backward_kernel,
+        name="backward",
+        out_shape=(
+            shape((tokens, width), low),
+            shape((tokens, width), wide),
+            shape((3, units * 8, lanes), low),
+            shape((lanes, n_all), wide),
+            shape((n_query, lanes), wide),
+            shape((8, lanes), wide),
+        ),
+        in_specs=[pl.BlockSpec(memory_space=pltpu.MemorySpace.SMEM)]
+        + [pl.BlockSpec(memory_space=VMEM)]
+        + [pl.BlockSpec(memory_space=HBM)] * 4
+        + [pl.BlockSpec(memory_space=VMEM)] * 10,
+        out_specs=[
+            pl.BlockSpec(memory_space=VMEM),
+            pl.BlockSpec(memory_space=VMEM),
+            pl.BlockSpec(memory_space=HBM),
+            pl.BlockSpec(memory_space=VMEM),
+            pl.BlockSpec(memory_space=VMEM),
+            pl.BlockSpec(memory_space=VMEM),
+        ],
+        scratch_shapes=[
+            pltpu.SemaphoreType.DMA((128,)),
+            pltpu.SemaphoreType.DMA((128,)),
+            vm((tokens, width), low),
+            vm((tokens, width), low),
+            vm((tokens, width), wide),
+            vm((n_query, tokens), low),
+            vm((8, n_query, 2 * lanes), low),
+            vm((tokens, n_query), low),
+            vm((tokens, n_all), low),
+            vm((width, tokens), low),
+            vm((16, lanes, n_all), low),
+            vm((keys, HEAD_SIZE), wide),
+            vm((keys, HEAD_SIZE), wide),
+            vm((4, tokens, kv_all.shape[1]), low),
+            vm((3, tokens, kv_all.shape[1]), low),
+            vm((tokens, width), low),
+            vm((tokens, width), low),
+            vm((8, width), wide),
+            vm((16, 8, lanes), wide),
+            vm((width, n_all), low),
+            vm((n_query, width), low),
+        ]
+        + token_scratch(tokens, width)
+        + plane_scratch((lanes, n_query))
+        + plane_scratch((lanes, n_all - n_query))
+        + plane_scratch((n_query, lanes)),
+        compiler_params=pltpu.CompilerParams(
+            collective_id=3, has_side_effects=True, vmem_limit_bytes=63 << 20
+        ),
+    )(
+        lengths, gn, part_b, g3, qkv_all, out_all, gain_all, hidden, states, gy, normed_one, q_rot,
+        kv_all, mixed, cosine, sine,
+    )
+
+
+def pick(c, table):
+    value = table[0]
+    for i in range(1, 4):
+        value = jnp.where(c == i, table[i], value)
+    return value
+
+
+NEAREST = ((0, 1, 2, 3), (1, 0, 2, 3), (2, 3, 1, 0), (3, 2, 1, 0))
+
+
+def forward_kernel(
+    lengths, states, gains, qkv, out_w, w3, gy, cosine, sine,
+    qkv_out, out_out, gain_out, hidden_out, normed_out, q_out, kv_out, mixed_out, part_out, g3, gn,
+    send, recv, qkv_all, out_all, gain_all, hidden, normed_one, q_rot, kv_all, mixed, part_b, gn_own,
+    unit_out, unit_in, unit_own, scaled, w3_all, gy_all, nt_all, act, both, act_t, both_t, part_g,
+    kv_own, pair_out, pair_in, nt, near, x_in, came,
+):
+    pos = position()
+    t, c, y, e = pos
+    low, wide = jnp.bfloat16, jnp.float32
+    wires = Wires(send, recv)
+    d = y * 2 + e
+    me = c * 4 + d
+    here, beside, over = (t, c, d), (t, c, y * 2 + 1 - e), (1 - t, c, d)
+    peers = [(True, over)]
+    for i in range(1, 16):
+        q = lax.rem(me + i, 16)
+        peers.append((True, (t, q // 4, lax.rem(q, 4))))
+    greet(peers)
+    tokens, width = states.shape
+    half = width // 2
+    block, n_all = qkv.shape
+    n_query = q_rot.shape[1]
+    n_key = (n_all - n_query) // 2
+    lanes = out_w.shape[1]
+    units = g3.shape[2]
+    kept_out = []
+
+    def save(src, dst):
+        kept_out.append(wires.fetch(wires.index(), src, dst))
+
+    def lane_block(q, size=lanes):
+        return pl.ds(pl.multiple_of(q * size, 128), size)
+
+    gain_id = [wires.index() for _ in range(16)]
+    for i in range(1, 16):
+        q = lax.rem(me + i, 16)
+        wires.push(
+            gain_id[i], lambda: gains, lambda: gain_all.at[:, lane_block(me)],
+            (t, q // 4, lax.rem(q, 4)),
+        )
+    fetch_gain = wires.fetch(wires.index(), gains, gain_all.at[:, lane_block(me)])
+    g_qkv = [
+        plane_gather(wires, pos, lambda: qkv, lambda k, f: rows(qkv_all, (k * 4 + f) * block, block))
+    ]
+    g_out = [
+        plane_gather(
+            wires, pos, lambda: out_w, lambda k, f: out_all.at[:, lane_block(k * 4 + f)]
+        )
+    ]
+    g_unit = [
+        unit_scatter(
+            wires, pos,
+            lambda q: w3.at[:, pl.ds(pl.multiple_of(q * units, 16), units)],
+            lambda k, f: w3_all.at[:, pl.ds(0, units), lane_block(k * 4 + f)],
+        )
+    ]
+
+    def spot(ref):
+        return lambda f, k, h: ref.at[
+            pl.ds(pl.multiple_of((k * 2 + f) * tokens, 16), tokens), lane_block(h, half)
+        ]
+
+    g_gy = [token_gather(wires, pos, None, spot(gy_all), lambda h: gy.at[:, lane_block(h, half)])]
+    advance(g_qkv)
+    advance(g_gy)
+    w3_all[:, units:, :] = jnp.zeros_like(w3_all[:, units:, :])
+
+    def scale_rows(r):
+        x = states[r].astype(wide)
+        scaled[r] = x * lax.rsqrt(jnp.mean(x * x, axis=-1, keepdims=True) + EPS)
+
+    by_rows(tokens, 16, scale_rows)
+    advance(g_qkv)
+    advance(g_out)
+    advance(g_gy)
+    advance(g_qkv)
+    advance(g_out)
+    advance(g_gy)
+    advance(g_qkv)
+    advance(g_out)
+    advance(g_gy)
+    while g_qkv:
+        advance(g_qkv)
+    fetch_gain.wait()
+    for i in range(1, 16):
+        q = lax.rem(me + 16 - i, 16)
+        wires.arrive(gain_id[i], lambda: gain_all.at[:, lane_block(q)])
+    gain_one = gain_all[...].astype(wide)[0:1]
+    gain_two = gain_all[...].astype(wide)[1:2]
+
+    save(qkv_all, qkv_out)
+    save(gain_all, gain_out)
+
+    def norm_one(r):
+        normed_one[r] = (scaled[r] * gain_one).astype(low)
+
+    by_rows(tokens, 16, norm_one)
+
+    def turned(x):
+        return x * cosine[...] + swap_halves(x) * sine[...]
+
+    tail = dot_nn(normed_one[...], qkv_all[:, n_query:])
+    kv_own[:, :n_key] = turned(tail[:, :n_key]).astype(low)
+    kv_own[:, n_key:] = tail[:, n_key:].astype(low)
+    kv_all[pl.ds(pl.multiple_of(c * tokens, 16), tokens)] = kv_own[...]
+    kv_id = [wires.index() for _ in range(3)]
+    for i in range(3):
+        k = lax.rem(c + i + 1, 4)
+        wires.push(kv_id[i], lambda: kv_own, lambda: rows(kv_all, c * tokens, tokens), (t, k, d))
+    advance(g_unit)
+
+    def project(j, carry):
+        where = pl.ds(pl.multiple_of(j * 256, 256), 256)
+        two = dot_nn(normed_one[...], qkv_all[:, where])
+        for h in range(2):
+            slab = pl.ds(pl.multiple_of(j * 256 + h * 128, 128), 128)
+            q_rot[:, slab] = turned(two[:, h * 128 : (h + 1) * 128]).astype(low)
+        return carry
+
+    lax.fori_loop(0, n_query // 256, project, 0)
+    advance(g_out)
+    for i in range(3):
+        k = lax.rem(c + 3 - i, 4)
+        wires.arrive(kv_id[i], lambda: rows(kv_all, k * tokens, tokens))
+    q_pos = c * tokens + lax.broadcasted_iota(jnp.int32, (tokens, kv_all.shape[0]), 0)
+    k_pos = lax.broadcasted_iota(jnp.int32, (tokens, kv_all.shape[0]), 1)
+    allowed = (k_pos <= q_pos) & (k_pos < lengths[0])
+    pairs = n_query // 256
+    for g in range(2):
+        keys = kv_all[:, g * HEAD_SIZE : (g + 1) * HEAD_SIZE]
+        values = kv_all[:, n_key + g * HEAD_SIZE : n_key + (g + 1) * HEAD_SIZE]
+
+        def pair(j, carry, g=g, keys=keys, values=values):
+            slab = pl.ds(pl.multiple_of((g * pairs + j) * 128, 128), 128)
+            q_two = q_rot[:, slab]
+            both_heads = []
+            for h in range(2):
+                probs = head_probs(q_two[:, h * HEAD_SIZE : (h + 1) * HEAD_SIZE], keys, allowed)
+                both_heads.append(dot_nn(probs.astype(low), values))
+            mixed[:, slab] = jnp.concatenate(both_heads, axis=1).astype(low)
+            return carry
+
+        lax.fori_loop(0, pairs, pair, 0)
+        if g == 0:
+            advance(g_out)
+    save(kv_all, kv_out)
+    save(q_rot, q_out)
+    save(mixed, mixed_out)
+    save(normed_one, normed_out)
+    while g_out:
+        advance(g_out)
+    advance(g_unit)
+    save(out_all, out_out)
+    pair_id = [wires.index() for _ in range(4)]
+    for i in range(4):
+        for j in range(2):
+            where = pl.ds(i * (width // 4) + j * (width // 8), width // 8)
+            pair_out[:, where] = dot_nn(mixed[...], out_all[:, where]).astype(low)
+        piece = pl.ds(i * (width // 4), width // 4)
+        wires.push(pair_id[i], lambda p=piece: pair_out.at[:, p], lambda p=piece: pair_in.at[:, p], over)
+    advance(g_unit, 2)
+    for i in range(4):
+        piece = pl.ds(i * (width // 4), width // 4)
+        wires.arrive(pair_id[i], lambda: pair_in.at[:, piece])
+
+    def norm_two(r):
+        total = states[r].astype(wide) + (pair_out[r].astype(wide) + pair_in[r].astype(wide))
+        hidden[r] = total
+        factor = lax.rsqrt(jnp.mean(total * total, axis=-1, keepdims=True) + EPS)
+        nt[r] = (total * factor * gain_two).astype(low)
+
+    by_rows(tokens, 16, norm_two)
+    save(hidden, hidden_out)
+
+    gathers = []
+    for source, target in ((nt, nt_all),):
+        at = spot(target)
+        z_id, x_id, e_id, f_id = [[wires.index() for _ in range(4)][0] for _ in range(4)]
+        gathers.append((at, z_id, x_id, e_id, f_id))
+        own_half = lambda h, source=source: source.at[:, lane_block(h, half)]
+        for i in (3, 1, 2):
+            k = lax.rem(c + i, 4)
+            wires.push(
+                wires.index(), lambda own=own_half: own(t), lambda at=at: at(e, c, t), (t, k, d),
+                lands=z_id + c,
+            )
+        wires.push(e_id + c, lambda own=own_half: own(t), lambda at=at: at(e, c, t), beside)
+        wires.push(f_id + c, lambda own=own_half: own(1 - t), lambda at=at: at(e, c, 1 - t), beside)
+    at_home = pl.ds(pl.multiple_of((c * 2 + e) * tokens, 16), tokens)
+    nt_all[at_home] = nt[...]
+    advance(g_unit, 4)
+    while g_gy:
+        advance(g_gy)
+
+    def nearest(j):
+        return pick(c, [sum_of(j, NEAREST[i]) for i in range(4)])
+
+    def sum_of(j, order):
+        value = order[0]
+        for i in range(1, 4):
+            value = jnp.where(j == i, order[i], value)
+        return value
+
+    def stage_one(j):
+        k = nearest(j)
+        for at, z_id, x_id, e_id, f_id in gathers:
+            wires.arrive(z_id + k, lambda: at(e, k, t))
+            wires.copy(x_id + k, at(e, k, t), at(e, k, t), over).start()
+            wires.copy(e_id + k, at(e, k, t), at(e, k, t), beside).start()
+
+    def stage_two(j):
+        k = nearest(j)
+        for at, z_id, x_id, e_id, f_id in gathers:
+
+            def act():
+                wires.arrive(x_id + k, lambda: at(e, k, 1 - t))
+                wires.copy(f_id + k, at(e, k, 1 - t), at(e, k, 1 - t), beside).start()
+
+            pl.when(j > 0)(act)
+        for at, z_id, x_id, e_id, f_id in gathers:
+            wires.arrive(e_id + k, lambda: at(1 - e, k, t))
+            wires.arrive(f_id + k, lambda: at(1 - e, k, 1 - t))
+
+    n_id = [wires.index() for _ in range(4)][0]
+    r_id = [wires.index() for _ in range(4)][0]
+
+    def part_rows(k, f):
+        return part_g.at[pl.ds(pl.multiple_of((k * 2 + f) * tokens, 16), tokens)]
+
+    mine, other = lane_block(t, half), lane_block(1 - t, half)
+
+    def stage_three(j):
+        k = nearest(j)
+        wires.arrive(n_id + k, lambda: near.at[k])
+        ours = part_rows(k, e)
+
+        def away(r):
+            total = ours[r, other].astype(wide) + near[k, r, other].astype(wide)
+            near[k, r, other] = total.astype(low)
+
+        by_rows(tokens, 16, away)
+        wires.copy(r_id + k, near.at[k, :, other], x_in.at[k], over).start()
+
+    def kept(k, r):
+        return (
+            part_rows(k, e)[r, mine].astype(wide)
+            + near[k, r, mine].astype(wide)
+            + x_in[k, r].astype(wide)
+        )
+
+    s_id = [wires.index() for _ in range(4)][0]
+
+    def stage_four(j):
+        k = nearest(j)
+        wires.arrive(r_id + k, lambda: x_in.at[k])
+
+        def add(r):
+            near[k, r, mine] = kept(k, r).astype(low)
+
+        by_rows(tokens, 16, add)
+        i = lax.rem(k - c + 4, 4)
+        wires.copy(s_id + i, near.at[k, :, mine], came.at[i - 1], (t, k, d)).start()
+
+    def swiglu(j, carry):
+        stage_two(j)
+        k = nearest(j)
+        where = pl.ds(pl.multiple_of(k * 2 * tokens, 16), 2 * tokens)
+        x = nt_all[where]
+        gate = times_transposed(x, w3_all[0])
+        up = times_transposed(x, w3_all[1])
+        grad_act = times_transposed(gy_all[where], w3_all[2])
+        sigma = jax.nn.sigmoid(gate)
+        swish = gate * sigma
+        act[where] = (swish * up).astype(low)
+        wide_units = gate.shape[1]
+        both[where, :wide_units] = (
+            grad_act * up * (sigma * (1.0 + gate * (1.0 - sigma)))
+        ).astype(low)
+        both[where, wide_units:] = (grad_act * swish).astype(low)
+        for i in range(4):
+            piece = slice(i * (width // 4), (i + 1) * (width // 4))
+            part_g[where, piece] = (
+                dot_nn(both[where, :wide_units], w3_all[0, :, piece])
+                + dot_nn(both[where, wide_units:], w3_all[1, :, piece])
+            ).astype(low)
+        wires.copy(n_id + k, part_rows(k, 1 - e), near.at[k], beside).start()
+        for i in range(4):
+            piece = slice(i * (width // 4), (i + 1) * (width // 4))
+            part_b[where, piece] = dot_nn(act[where], w3_all[2, :, piece]).astype(low)
+        pl.when(j > 0)(lambda: stage_three(j - 1))
+        pl.when(j > 2)(lambda: stage_four(j - 2))
+        return carry
+
+    for j in range(1, 4):
+        stage_one(j)
+    while g_unit:
+        advance(g_unit)
+    lax.fori_loop(0, 4, swiglu, 0)
+    save(part_b, part_out)
+    stage_three(3)
+    for k in range(4):
+        away = c != k
+        for at, z_id, x_id, e_id, f_id in gathers:
+            half_at = lambda h, k=k, at=at: at(e, k, h)
+            wires.owe(x_id + k, lambda f=half_at: f(t), away)
+            wires.owe(e_id + k, lambda f=half_at: f(t), away)
+            wires.owe(f_id + k, lambda f=half_at: f(1 - t), away)
+        wires.owe(n_id + k, lambda k=k: part_rows(k, 1 - e))
+        wires.owe(r_id + k, lambda k=k: near.at[k, :, other])
+    for i in (1, 2, 3):
+        k = lax.rem(c + i, 4)
+        wires.owe(s_id + i, lambda k=k: near.at[k, :, mine])
+    stage_four(2)
+    act_t[...] = act[...].T
+    both_t[...] = both[...].T
+
+    def unit_grads(k, yy, place):
+        where = lane_block(k * 2 + yy, 256)
+        wide_units = act_t.shape[0]
+        two = dot_nn(both_t[...], nt_all[:, where]).astype(low)
+        place[k, 0] = two[:units]
+        place[k, 1] = two[wide_units : wide_units + units]
+        place[k, 2] = dot_nn(act_t[...], gy_all[:, where]).astype(low)[:units]
+
+    u_id = [wires.index() for _ in range(4)][0]
+    across = (t, c, (1 - y) * 2 + e)
+
+    def send_units(k, carry):
+        unit_grads(k, 1 - y, unit_out)
+        wires.copy(u_id + k, unit_out.at[k], unit_in.at[k], across).start()
+        return carry
+
+    lax.fori_loop(0, 2, send_units, 0)
+    stage_four(3)
+    lax.fori_loop(2, 4, send_units, 0)
+    for k in range(4):
+        wires.owe(u_id + k, lambda k=k: unit_out.at[k])
+
+    def keep_units(k, carry):
+        unit_grads(k, y, unit_own)
+        return carry
+
+    lax.fori_loop(0, 2, keep_units, 0)
+    wires.arrive(r_id + c, lambda: x_in.at[c])
+    for i in (3, 1, 2):
+        wires.arrive(s_id + i, lambda: came.at[i - 1])
+
+    def done(r):
+        total = kept(c, r)
+        for i in range(3):
+            total = total + came[i, r].astype(wide)
+        gn_own[r, mine] = total.astype(low)
+
+    by_rows(tokens, 16, done)
+    last = wires.index()
+    wires.push(last, lambda: gn_own.at[:, mine], lambda: gn_own.at[:, mine], over)
+    lax.fori_loop(2, 4, keep_units, 0)
+    g_save = wires.index(), wires.index(), wires.index(), wires.index()
+    saves = []
+    for k in range(4):
+        wires.arrive(u_id + k, lambda: unit_in.at[k])
+        for m in range(3):
+
+            def add(r):
+                both_y = unit_own[k, m, r].astype(wide) + unit_in[k, m, r].astype(wide)
+                unit_own[k, m, r] = both_y.astype(low)
+
+            by_rows(units, 16, add)
+        saves.append(wires.fetch(g_save[k], unit_own.at[k], g3.at[k]))
+    wires.arrive(last, lambda: gn_own.at[:, other])
+    saves.append(wires.fetch(wires.index(), gn_own, gn))
+    for copy in saves + kept_out:
+        copy.wait()
+    wires.drain()
+
+
+def forward_call(lengths, states, gains, qkv, out_w, w3, gy, cosine, sine):
+    shape = jax.ShapeDtypeStruct
+    low, wide = jnp.bfloat16, jnp.float32
+    tokens, width = states.shape
+    n_query, lanes = out_w.shape
+    n_all = qkv.shape[1]
+    units = w3.shape[1] // 8
+    padded = -(-units // 128) * 128
+    all_tokens = tokens * 8
+    half = width // 2
+    vm = pltpu.VMEM
+    return pl.pallas_call(
+        forward_kernel,
+        name="forward",
+        out_shape=(
+            shape((width, n_all), low),
+            shape((n_query, width), low),
+            shape((16, width), low),
+            shape((tokens, width), wide),
+            shape((tokens, width), low),
+            shape((tokens, n_query), low),
+            shape((tokens * 4, n_all - n_query), low),
+            shape((tokens, n_query), low),
+            shape((all_tokens, width), low),
+            shape((4, 3, units, width // 8), low),
+            shape((tokens, width), low),
+        ),
+        in_specs=[pl.BlockSpec(memory_space=pltpu.MemorySpace.SMEM), pl.BlockSpec(memory_space=VMEM)]
+        + [pl.BlockSpec(memory_space=HBM)] * 5
+        + [pl.BlockSpec(memory_space=VMEM)] * 2,
+        out_specs=[pl.BlockSpec(memory_space=HBM)] * 11,
+        scratch_shapes=[
+            pltpu.SemaphoreType.DMA((200,)),
+            pltpu.SemaphoreType.DMA((200,)),
+            vm((width, n_all), low),
+            vm((n_query, width), low),
+            vm((16, width), low),
+            vm((tokens, width), wide),
+            vm((tokens, width), low),
+            vm((tokens, n_query), low),
+            vm((tokens * 4, n_all - n_query), low),
+            vm((tokens, n_query), low),
+            vm((all_tokens, width), low),
+            vm((tokens, width), low),
+            vm((4, 3, units, width // 8), low),
+            vm((4, 3, units, width // 8), low),
+            vm((4, 3, units, width // 8), low),
+            vm((tokens, width), wide),
+            vm((3, padded, width), low),
+            vm((all_tokens, width), low),
+            vm((all_tokens, width), low),
+            vm((all_tokens, padded), low),
+            vm((all_tokens, 2 * padded), low),
+            vm((padded, all_tokens), low),
+            vm((2 * padded, all_tokens), low),
+            vm((all_tokens, width), low),
+            vm((tokens, n_all - n_query), low),
+            vm((tokens, width), low),
+            vm((tokens, width), low),
+            vm((tokens, width), low),
+            vm((4, tokens, width), low),
+            vm((4, tokens, half), low),
+            vm((3, tokens, half), low),
+        ],
+        compiler_params=pltpu.CompilerParams(
+            collective_id=1, has_side_effects=True, vmem_limit_bytes=63 << 20
+        ),
+    )(lengths, states, gains, qkv, out_w, w3, gy, cosine, sine)
+
+
+def plane_shards(
+    states, lengths, first_gain, w_query, key_matrix, value_matrix, w_out, second_gain,
+    w_gate, w_up, w_down, cotangent,
+):
+    low, wide = jnp.bfloat16, jnp.float32
+    tokens = states.shape[1]
+    positions = lax.axis_index("ctx") * tokens + jnp.arange(tokens, dtype=jnp.int32)
+    cosine, sine = rope_tables(positions, HEAD_SIZE // 2)
+    lane = jnp.arange(2 * HEAD_SIZE)
+    turn = jnp.where((lane % HEAD_SIZE) < HEAD_SIZE // 2, -1.0, 1.0)
+    cosine = jnp.tile(cosine[:, 0], (1, 4))
+    sine = jnp.tile(sine[:, 0], (1, 4)) * turn[None, :]
+    valid = (positions < lengths[0])[:, None]
+    grad_y = jnp.where(valid, cotangent[0], jnp.zeros((), low))
+    n_query, n_key = w_query.shape[1], key_matrix.shape[1]
+    lanes = w_out.shape[1]
+    qkv = jnp.concatenate([w_query, key_matrix, value_matrix], axis=1)
+    gains = jnp.concatenate(
+        [first_gain[None], second_gain[None], jnp.zeros((14, lanes), low)], axis=0
+    )
+    w3 = jnp.stack([w_gate.T, w_up.T, w_down])
+    qkv_all, out_all, gain_all, hidden, normed_one, q_rot, kv_all, mixed, part_b, g3, gn = (
+        forward_call(lengths, states[0], gains, qkv, w_out, w3, grad_y, cosine, sine)
+    )
+    layer_out, grad_states, g3, gq, go, gain = backward_call(
+        lengths, gn, part_b, g3, qkv_all, out_all, gain_all, hidden, states[0], grad_y,
+        normed_one, q_rot, kv_all, mixed, cosine, sine,
+    )
+    return (
+        layer_out[None],
+        grad_states[None],
+        gain[0],
+        gq[:, :n_query],
+        gq[:, n_query : n_query + n_key],
+        gq[:, n_query + n_key :],
+        go,
+        gain[1],
+        g3[0].T.astype(wide),
+        g3[1].T.astype(wide),
+        g3[2].astype(wide),
+    )
+
+
+def fits(mesh):
+    return dict(mesh.shape) == {"tensor": 2, "ctx": 4, "dp": 4}
+
+
 def solution(mesh):
     placed = (
         P("dp", "ctx", None),
@@ -334,7 +1627,7 @@
         P("dp", "ctx", None),
     )
     return jax.shard_map(
-        shards,
+        plane_shards if fits(mesh) else shards,
         mesh=mesh,
         in_specs=placed,
         out_specs=(

time: 1660 us -> 394 us (0.24)
  waiting for transfers between devices: 1320 us -> 0 us
  Pallas kernels: 0 us -> 369 us
  blocking collectives: 159 us -> 0 us
  matrix products: 122 us -> 0 us
    reduce_scatter x9 -> x0, waiting for transfers between devices: 993 us -> none  [the longest x1 231 us: shards(): lax.psum_scatter(grad_up, ('ctx', 'dp'), scatter_dimension=0, tiled=True)]
    pallas_call x0 -> x2, Pallas kernels: none -> 369 us  [the longest x1 216 us: forward_call(): pl.pallas_call(forward_kernel, name='forward', out_shape=(shape((width, n...]
    all_gather x5 -> x0, waiting for transfers between devices: 275 us -> none  [the longest x1 94 us: shards(): lax.all_gather(w_gate, ('ctx', 'dp'), axis=0, tiled=True)]
    dot_general x27 -> x0, matrix products: 122 us -> none  [the longest x7 44.3 us: transposed_times(): lax.dot_general(left, right, (((0,), (0,)), ((), ())), preferred_element_...]
    all_gather x6 -> x0, blocking collectives: 106 us -> none  [the longest x1 22.6 us: shards(): lax.all_gather(key_matrix, ('ctx', 'dp'), axis=0, tiled=True)]
    psum x3 -> x0, waiting for transfers between devices: 54 us -> none  [the longest x1 33.2 us: shards(): lax.psum(times_transposed(grad_gate_low, full_gate) + times_transposed(gr...]
    unnamed x1 -> x0, blocking collectives: 52.7 us -> none
  transfers between devices with their start and end apart: 17 -> 0, of which waited for: 14 -> 0; matrix products, arithmetic and copies ran while one was open for 6% -> 0% of each run, Pallas kernels for 0% -> 0%
where the time goes in v1:
time: 394 us; the launch traced here: 393 us
  Pallas kernels  369 us (94%)
  local copies, waits for them, and re-layouts  11.9 us (3%)
  other arithmetic  10.4 us (3%)
    pallas_call x1, Pallas kernels, forward_call(): pl.pallas_call(forward_kernel, name='forward', out_shape=(shape((width, n...  216 us
    pallas_call x1, Pallas kernels, backward_call(): pl.pallas_call(backward_kernel, name='backward', out_shape=(shape((tokens...  154 us

profile of v1, /device:TPU:8, one launch (start us, length us, event | category | flops | bytes accessed | tf_op | source)
XLA Modules:
  0.0 393.3 jit_solution(17882309515634496929)
XLA Ops:
  0.6 0.0 copy-start.2
  0.7 0.0 copy-start.1
  1.5 0.1 pad.8.clone
  1.5 1.3 maximum_maximum_fusion.gains
  2.9 0.1 multiply_sine_fusion
  3.0 0.1 copy.29
  3.1 0.6 broadcast_multiply_fusion.sine
  3.8 0.7 copy.30.cosine
  4.5 0.0 copy-start.3
  4.5 1.8 pad_maximum_fusion.1.qkv
  6.3 1.9 bitcast_select_fusion.gy
  8.3 0.0 copy-done.1
  8.3 0.3 copy.27
  8.6 0.0 copy-done.2
  8.6 0.3 copy.28
  9.0 0.0 copy-done.3
  9.0 1.6 pad_maximum_fusion.w3
  10.6 215.6 %forward.1 = (bf16[2048,1280]{1,0:T(8,128)(2,1)}, bf16[1024,2048]{1,0:T(8,128)(2,1)}, bf16[16,2048]{1,0:T(8,128)(2,1)}, f32[128,2048]{1,0:T(8,128)}, bf16[128,20...) custom-call(s32[1]{0:T(128)} %copy.37.lengths, ...), custom_call_target="tpu_custom_call" | custom-call | tf_op jit(solution)/shard_map/forward/pallas_call | solution.py:1508
  226.2 153.8 %backward.1 = (bf16[128,2048]{1,0:T(8,128)(2,1)}, f32[128,2048]{1,0:T(8,128)}, bf16[3,2816,128]{2,1,0:T(8,128)(2,1)}, f32[128,1280]{1,0:T(8,128)}, f32[1024,128]{1,0:T(8,128)}, /*index=5*/f32[8,128]{1,0:T(8,128)}) custom-call(s32[1]{0:T(128)} %copy.37.lengths, bf16[128,2048]{1,0:T(8,128)(2,1)} %get-tuple-element.28.gn, ...), custom_call_target="tpu_custom_call" | custom-call | tf_op jit(solution)/shard_map/backward/pallas_call | solution.py:1051
  380.0 1.3 slice_bitcast_fusion
  381.3 1.5 fusion.2
  382.8 1.9 slice.25
  384.7 2.9 bitcast_convert_fusion
  387.6 1.5 copy.33
  389.1 0.0 copy-start.5
  389.1 1.5 copy.32
  390.7 0.0 copy-done.5
  390.7 0.8 copy.38
  391.5 0.0 copy-done
  391.5 1.0 copy.39
  392.5 0.0 copy-done.4
  392.5 0.8 copy.40
  (9 shorter events, 0.0 us)
Async XLA Ops:
  0.6 8.0 %copy-start.2 = (bf16[128,2816]{1,0:T(8,128)(2,1)S(1)}, bf16[128,2816]{1,0:T(8,128)(2,1)}, u32[]{:S(2)}) copy-start(bf16[128,2816]{1,0:T(8,128)(2,1)} %param.21) | copy-start | bytes 2162692
  0.7 7.6 %copy-start.1 = (bf16[128,2816]{1,0:T(8,128)(2,1)S(1)}, bf16[128,2816]{1,0:T(8,128)(2,1)}, u32[]{:S(2)}) copy-start(bf16[128,2816]{1,0:T(8,128)(2,1)} %param.20) | copy-start | bytes 2162692
  4.5 4.5 %copy-start.3 = (bf16[2816,128]{1,0:T(8,128)(2,1)S(1)}, bf16[2816,128]{1,0:T(8,128)(2,1)}, u32[]{:S(2)}) copy-start(bf16[2816,128]{1,0:T(8,128)(2,1)} %param.22) | copy-start | bytes 2162692
  389.1 1.5 copy-start.5
  389.1 2.3 copy-start
  390.7 1.8 copy-start.4

commit v2 on v1

--- a/solution.py
+++ b/solution.py
@@ -651,7 +651,7 @@
     return hop, finish
 
 
-def token_scatter(wires, pos, part, out, scratch):
+def token_scatter(wires, pos, part, out, scratch, credit):
     t, c, y, e = pos
     near, own, x_in, came, extra = scratch
     wide = jnp.float32
@@ -666,21 +666,23 @@
     def begin(k, f):
         return pl.multiple_of((k * 2 + f) * tokens, 16)
 
+    pl.semaphore_wait(credit.at[0], 1)
     for k in ORDER:
         wires.push(
             e_id[k], lambda k=k: part.at[pl.ds(begin(k, 1 - e), tokens)],
             lambda k=k: near.at[k], (t, c, d_e),
         )
     fetch = [
-        wires.fetch(wires.index(), part.at[pl.ds(begin(k, e), tokens)], own.at[k]) for k in range(4)
+        wires.fetch(wires.index(), part.at[pl.ds(begin(k, e), tokens)], own(k)) for k in range(4)
     ]
     yield
+    pl.semaphore_wait(credit.at[1], 1)
     for k in ORDER:
         fetch[k].wait()
         wires.arrive(e_id[k], lambda: near.at[k])
 
         def away(r):
-            total = own[k, r, other].astype(wide) + near[k, r, other].astype(wide)
+            total = own(k)[r, other].astype(wide) + near[k, r, other].astype(wide)
             near[k, r, other] = total.astype(near.dtype)
 
         by_rows(tokens, 16, away)
@@ -691,7 +693,7 @@
 
     def value(k, r):
         return (
-            own[k, r, mine].astype(wide)
+            own(k)[r, mine].astype(wide)
             + near[k, r, mine].astype(wide)
             + x_in[k, r].astype(wide)
         )
@@ -702,6 +704,8 @@
     hop, finish = chain_sum(
         wires, pos, tokens, value, lambda k: near.at[k, :, mine], came, extra, done
     )
+    pl.when(c < 3)(lambda: pl.semaphore_wait(credit.at[2], 1))
+    pl.when(c > 0)(lambda: pl.semaphore_wait(credit.at[3], 1))
     for k in ORDER:
         wires.arrive(x_id[k], lambda: x_in.at[k])
         hop(k)
@@ -710,17 +714,6 @@
     wires.push(last, lambda: out.at[:, mine], lambda: out.at[:, mine], (1 - t, c, y * 2 + e))
     yield
     wires.arrive(last, lambda: out.at[:, other])
-
-
-def token_scratch(tokens, width):
-    low, half = jnp.bfloat16, width // 2
-    return [
-        pltpu.VMEM((4, tokens, width), low),
-        pltpu.VMEM((4, tokens, width), low),
-        pltpu.VMEM((4, tokens, half), low),
-        pltpu.VMEM((4, tokens, half), low),
-        pltpu.VMEM((tokens, half), low),
-    ]
 
 
 def plane_scatter(wires, pos, out_block, own_block, height, scratch, done):
@@ -778,27 +771,46 @@
     ]
 
 
-def unit_gather(wires, pos, sums, out):
+def unit_gather(wires, pos, grads, came, y_id, out):
     t, c, y, e = pos
-    units, lanes = sums.shape[2], out.shape[2]
+    wide = jnp.float32
+    units, lanes = came.shape[2], out.shape[2]
     me = c * 2 + e
     o_id = [wires.index() for _ in range(8)]
     here = pl.ds(pl.multiple_of(me * units, 16), units)
-    for i in range(1, 8):
-        q = lax.rem(me + i, 8)
-        wires.push(
-            o_id[i],
-            lambda q=q: sums.at[q // 2, :, :, pl.ds(pl.multiple_of((q % 2) * lanes, 128), lanes)],
-            lambda: out.at[:, here], (t, q // 2, y * 2 + q % 2),
-        )
-    fetch = wires.fetch(
-        wires.index(), sums.at[c, :, :, pl.ds(pl.multiple_of(e * lanes, 128), lanes)], out.at[:, here]
-    )
-    yield
-    for i in range(1, 8):
-        q = lax.rem(me + 8 - i, 8)
-        wires.arrive(o_id[i], lambda: out.at[:, pl.ds(pl.multiple_of(q * units, 16), units)])
-    fetch.wait()
+    fetch = []
+    for far in (1, 2, 3, 0):
+        k = lax.rem(c + far, 4)
+        wires.arrive(y_id + k, lambda: came.at[k])
+        where = pl.ds(pl.multiple_of((k * 2 + y) * 2 * lanes, 256), 2 * lanes)
+        for m in range(3):
+
+            def add(r):
+                both = grads[m, r, where].astype(wide) + came[k, m, r].astype(wide)
+                grads[m, r, where] = both.astype(grads.dtype)
+
+            by_rows(units, 16, add)
+        for f in range(2):
+            g = e if f == 0 else 1 - e
+            src = lambda k=k, g=g: grads.at[
+                :, pl.ds(0, units), pl.ds(pl.multiple_of(((k * 2 + y) * 2 + g) * lanes, 128), lanes)
+            ]
+            if far == 0 and f == 0:
+                fetch.append(wires.fetch(wires.index(), src(), out.at[:, here]))
+            else:
+                wires.push(o_id[far * 2 + f], src, lambda: out.at[:, here], (t, k, y * 2 + g))
+        yield
+    for far in (1, 2, 3, 0):
+        for f in range(2):
+            if far == 0 and f == 0:
+                continue
+            k = lax.rem(c + 4 - far, 4)
+            g = e if f == 0 else 1 - e
+            wires.arrive(
+                o_id[far * 2 + f],
+                lambda: out.at[:, pl.ds(pl.multiple_of((k * 2 + g) * units, 16), units)],
+            )
+    fetch[0].wait()
 
 
 def swap_halves(x):
@@ -831,282 +843,6 @@
                 parts.remove(part)
 
 
-def backward_kernel(
-    lengths, gn, part_b, g3, qkv_hbm, out_hbm, gain_all, hidden, states, gy, normed_one, q_rot, kv_all,
-    mixed, cosine, sine,
-    layer_out, grad_states, g3_out, gq_out, go_out, gain_out,
-    send, recv, grad_low, branch, grad_hidden, mixed_t, go_part, grad_mixed, gqkv, normed_t, gq_part,
-    dk, dv, kv_part, kv_in, pair_out, pair_in, gains, gain_in, qkv_all, out_all, *scratch,
-):
-    pos = position()
-    t, c, y, e = pos
-    low, wide = jnp.bfloat16, jnp.float32
-    wires = Wires(send, recv)
-    d = y * 2 + e
-    me = c * 4 + d
-    peers = [(True, (1 - t, c, d))]
-    for i in range(1, 16):
-        q = lax.rem(me + i, 16)
-        peers.append((True, (t, q // 4, lax.rem(q, 4))))
-    greet(peers)
-    tokens, width = states.shape
-    n_query = q_rot.shape[1]
-    n_key = kv_all.shape[1] // 2
-    lanes = go_out.shape[1]
-    rows_out = go_out.shape[0]
-    t_b, s_q, s_k, s_o = scratch[:5], scratch[5:9], scratch[9:13], scratch[13:17]
-    load_out = wires.fetch(wires.index(), out_hbm, out_all)
-    load_qkv = wires.fetch(wires.index(), qkv_hbm, qkv_all)
-
-    units = [unit_gather(wires, pos, g3, g3_out)]
-    second = [token_scatter(wires, pos, part_b, branch, t_b)]
-    advance(units)
-    mixed_t[...] = mixed[...].T
-    normed_t[...] = normed_one[...].T
-    advance(second)
-
-    gains[...] = jnp.zeros_like(gains)
-    gain_one = gain_all[...].astype(wide)[0:1]
-    gain_two = gain_all[...].astype(wide)[1:2]
-
-    def norm_two(r):
-        value, grad = norm_rows(gn[r].astype(wide), hidden[r], gain_two)
-        total = gy[r].astype(wide) + value
-        grad_hidden[r] = total
-        grad_low[r] = total.astype(low)
-        gains[1:2] += grad
-
-    by_rows(tokens, 16, norm_two)
-
-    def out_grad(j, carry):
-        where = pl.ds(pl.multiple_of(j * 2 * lanes, 256), 2 * lanes)
-        go_part[j] = dot_nn(mixed_t[...], grad_low[:, where]).astype(low)
-        return carry
-
-    lax.fori_loop(0, 8, out_grad, 0)
-    outs = [
-        plane_scatter(
-            wires, pos,
-            lambda k, yy: go_part.at[k * 2 + yy, :, pl.ds(pl.multiple_of((1 - e) * lanes, 128), lanes)],
-            lambda k, yy: go_part.at[k * 2 + yy, :, pl.ds(pl.multiple_of(e * lanes, 128), lanes)],
-            rows_out, s_o, lambda r, v: go_out.__setitem__(r, v),
-        )
-    ]
-    advance(outs)
-
-    load_out.wait()
-
-    def mix_grad(j, carry):
-        where = pl.ds(pl.multiple_of(j * 256, 256), 256)
-        grad_mixed[:, where] = times_transposed(grad_low[...], out_all[where, :]).astype(low)
-        return carry
-
-    lax.fori_loop(0, n_query // 256, mix_grad, 0)
-
-    q_pos = c * tokens + lax.broadcasted_iota(jnp.int32, (tokens, kv_all.shape[0]), 0)
-    k_pos = lax.broadcasted_iota(jnp.int32, (tokens, kv_all.shape[0]), 1)
-    allowed = (k_pos <= q_pos) & (k_pos < lengths[0])
-    scale = HEAD_SIZE ** (-0.5)
-    pairs = n_query // 256
-    for g in range(2):
-        keys = kv_all[:, g * HEAD_SIZE : (g + 1) * HEAD_SIZE]
-        values = kv_all[:, n_key + g * HEAD_SIZE : n_key + (g + 1) * HEAD_SIZE]
-        dk[...] = jnp.zeros_like(dk)
-        dv[...] = jnp.zeros_like(dv)
-
-        def pair(j, carry, g=g, keys=keys, values=values):
-            slab = pl.ds(pl.multiple_of((g * pairs + j) * 128, 128), 128)
-            q_two, m_two = q_rot[:, slab], grad_mixed[:, slab]
-            both = []
-            for h in range(2):
-                query = q_two[:, h * HEAD_SIZE : (h + 1) * HEAD_SIZE]
-                upstream = m_two[:, h * HEAD_SIZE : (h + 1) * HEAD_SIZE]
-                probs = head_probs(query, keys, allowed)
-                dprob = times_transposed(upstream, values)
-                delta = jnp.sum(probs * dprob, axis=-1, keepdims=True)
-                grad_scores = (probs * (dprob - delta)).astype(low)
-                both.append(dot_nn(grad_scores, keys))
-                dk[...] += transposed_times(grad_scores, query)
-                dv[...] += transposed_times(probs.astype(low), upstream)
-            grads = jnp.concatenate(both, axis=1) * scale
-            back = grads * cosine[...] - swap_halves(grads) * sine[...]
-            gqkv[:, slab] = back.astype(low)
-            return carry
-
-        lax.fori_loop(0, pairs, pair, 0)
-        for k in range(4):
-            block = slice(k * tokens, (k + 1) * tokens)
-            kv_part[k, :, g * HEAD_SIZE : (g + 1) * HEAD_SIZE] = (dk[block] * scale).astype(low)
-            kv_part[k, :, n_key + g * HEAD_SIZE : n_key + (g + 1) * HEAD_SIZE] = dv[block].astype(low)
-        advance(outs)
-
-    kv_id = [wires.index() for _ in range(3)]
-    for i in range(3):
-        k = lax.rem(c + i + 1, 4)
-        wires.push(kv_id[i], lambda k=k: kv_part.at[k], lambda i=i: kv_in.at[i], (t, k, d))
-
-    def q_grad(core, where):
-        def act(j, carry):
-            owner = j * 2 + core
-            here = pl.ds(pl.multiple_of(owner * lanes, 128), lanes)
-            gq_part[owner, :, where] = dot_nn(normed_t[here, :], gqkv[:, where]).astype(low)
-            return carry
-
-        lax.fori_loop(0, 8, act, 0)
-
-    def q_sums(where, scratches):
-        def done(r, value):
-            gq_out[r, where] = value
-
-        return plane_scatter(
-            wires, pos,
-            lambda k, yy: gq_part.at[k * 4 + yy * 2 + 1 - e, :, where],
-            lambda k, yy: gq_part.at[k * 4 + yy * 2 + e, :, where],
-            gq_out.shape[0], scratches, done,
-        )
-
-    first, rest = slice(0, n_query), slice(n_query, n_query + 2 * n_key)
-    q_grad(1 - e, first)
-    queries = [q_sums(first, s_q)]
-    advance(queries)
-    q_grad(e, first)
-    for _ in range(4):
-        advance(queries)
-    total = kv_part[c].astype(wide)
-    for i in range(3):
-        wires.arrive(kv_id[i], lambda: kv_in.at[i])
-        total = total + kv_in[i].astype(wide)
-    key_grads = total[:, :n_key]
-    key_grads = key_grads * cosine[...] - swap_halves(key_grads) * sine[...]
-    gqkv[:, n_query : n_query + n_key] = key_grads.astype(low)
-    gqkv[:, n_query + n_key :] = total[:, n_key:].astype(low)
-    q_grad(1 - e, rest)
-    others = [q_sums(rest, s_k)]
-    advance(others)
-    q_grad(e, rest)
-    load_qkv.wait()
-
-    def normed_grad(j, carry):
-        where = pl.ds(pl.multiple_of(j * 256, 256), 256)
-        pair_out[:, where] = times_transposed(gqkv[...], qkv_all[where, :]).astype(low)
-        return carry
-
-    lax.fori_loop(0, width // 256, normed_grad, 0)
-    p_id = wires.index()
-    wires.push(p_id, lambda: pair_out, lambda: pair_in, (1 - t, c, d))
-    for _ in range(4):
-        advance(others)
-    advance(second)
-    wires.arrive(p_id, lambda: pair_in)
-
-    def norm_one(r):
-        upstream = pair_out[r].astype(wide) + pair_in[r].astype(wide)
-        value, grad = norm_rows(upstream, states[r].astype(wide), gain_one)
-        grad_states[r] = grad_hidden[r] + value
-        gains[0:1] += grad
-
-    by_rows(tokens, 16, norm_one)
-    g_id = [wires.index() for _ in range(16)]
-
-    def gain_block(q):
-        return gains.at[:, pl.ds(pl.multiple_of(q * lanes, 128), lanes)]
-
-    for i in range(1, 16):
-        q = lax.rem(me + i, 16)
-        wires.push(
-            g_id[i], lambda q=q: gain_block(q), lambda i=i: gain_in.at[i],
-            (t, q // 4, lax.rem(q, 4)),
-        )
-    while second or outs or queries or others:
-        advance(outs)
-        advance(queries)
-        advance(others)
-        advance(second)
-    advance(units)
-
-    def finish(r):
-        layer_out[r] = (hidden[r] + branch[r].astype(wide)).astype(low)
-
-    by_rows(tokens, 16, finish)
-    gain = gains[:, pl.ds(pl.multiple_of(me * lanes, 128), lanes)]
-    for i in range(1, 16):
-        wires.arrive(g_id[i], lambda: gain_in.at[i])
-        gain = gain + gain_in[i]
-    gain_out[...] = gain
-    wires.drain()
-
-
-def backward_call(
-    lengths, gn, part_b, g3, qkv_all, out_all, gain_all, hidden, states, gy, normed_one, q_rot, kv_all,
-    mixed, cosine, sine,
-):
-    shape = jax.ShapeDtypeStruct
-    low, wide = jnp.bfloat16, jnp.float32
-    units = g3.shape[2]
-    tokens, width = states.shape
-    n_query, keys = q_rot.shape[1], kv_all.shape[0]
-    n_all = qkv_all.shape[1]
-    lanes = width // 16
-    vm = pltpu.VMEM
-    return pl.pallas_call(
-        backward_kernel,
-        name="backward",
-        out_shape=(
-            shape((tokens, width), low),
-            shape((tokens, width), wide),
-            shape((3, units * 8, lanes), low),
-            shape((lanes, n_all), wide),
-            shape((n_query, lanes), wide),
-            shape((8, lanes), wide),
-        ),
-        in_specs=[pl.BlockSpec(memory_space=pltpu.MemorySpace.SMEM)]
-        + [pl.BlockSpec(memory_space=VMEM)]
-        + [pl.BlockSpec(memory_space=HBM)] * 4
-        + [pl.BlockSpec(memory_space=VMEM)] * 10,
-        out_specs=[
-            pl.BlockSpec(memory_space=VMEM),
-            pl.BlockSpec(memory_space=VMEM),
-            pl.BlockSpec(memory_space=HBM),
-            pl.BlockSpec(memory_space=VMEM),
-            pl.BlockSpec(memory_space=VMEM),
-            pl.BlockSpec(memory_space=VMEM),
-        ],
-        scratch_shapes=[
-            pltpu.SemaphoreType.DMA((128,)),
-            pltpu.SemaphoreType.DMA((128,)),
-            vm((tokens, width), low),
-            vm((tokens, width), low),
-            vm((tokens, width), wide),
-            vm((n_query, tokens), low),
-            vm((8, n_query, 2 * lanes), low),
-            vm((tokens, n_query), low),
-            vm((tokens, n_all), low),
-            vm((width, tokens), low),
-            vm((16, lanes, n_all), low),
-            vm((keys, HEAD_SIZE), wide),
-            vm((keys, HEAD_SIZE), wide),
-            vm((4, tokens, kv_all.shape[1]), low),
-            vm((3, tokens, kv_all.shape[1]), low),
-            vm((tokens, width), low),
-            vm((tokens, width), low),
-            vm((8, width), wide),
-            vm((16, 8, lanes), wide),
-            vm((width, n_all), low),
-            vm((n_query, width), low),
-        ]
-        + token_scratch(tokens, width)
-        + plane_scratch((lanes, n_query))
-        + plane_scratch((lanes, n_all - n_query))
-        + plane_scratch((n_query, lanes)),
-        compiler_params=pltpu.CompilerParams(
-            collective_id=3, has_side_effects=True, vmem_limit_bytes=63 << 20
-        ),
-    )(
-        lengths, gn, part_b, g3, qkv_all, out_all, gain_all, hidden, states, gy, normed_one, q_rot,
-        kv_all, mixed, cosine, sine,
-    )
-
-
 def pick(c, table):
     value = table[0]
     for i in range(1, 4):
@@ -1117,12 +853,13 @@
 NEAREST = ((0, 1, 2, 3), (1, 0, 2, 3), (2, 3, 1, 0), (3, 2, 1, 0))
 
 
-def forward_kernel(
+def layer_kernel(
     lengths, states, gains, qkv, out_w, w3, gy, cosine, sine,
-    qkv_out, out_out, gain_out, hidden_out, normed_out, q_out, kv_out, mixed_out, part_out, g3, gn,
-    send, recv, qkv_all, out_all, gain_all, hidden, normed_one, q_rot, kv_all, mixed, part_b, gn_own,
-    unit_out, unit_in, unit_own, scaled, w3_all, gy_all, nt_all, act, both, act_t, both_t, part_g,
-    kv_own, pair_out, pair_in, nt, near, x_in, came,
+    layer_out, grad_states, g3_out, gq_out, go_out, gain_out, qkv_kept, part_b,
+    send, recv, credit, qkv_all, out_all, gain_all, hidden, normed_one, q_rot, kv_all, mixed, gn_own,
+    w3_all, gy_all, nt_all, act_t, part_g, stage_b, unit_in, kv_own, pair_out, pair_in, nt,
+    near, x_in, came, grad_hidden, grad_low, branch, mixed_t, grad_mixed, gqkv, normed_t, gq_part,
+    dk, dv, kv_part, kv_in, gains_sum, gain_in, *scratch,
 ):
     pos = position()
     t, c, y, e = pos
@@ -1142,11 +879,8 @@
     n_query = q_rot.shape[1]
     n_key = (n_all - n_query) // 2
     lanes = out_w.shape[1]
-    units = g3.shape[2]
-    kept_out = []
-
-    def save(src, dst):
-        kept_out.append(wires.fetch(wires.index(), src, dst))
+    units = unit_in.shape[2]
+    scaled = grad_hidden
 
     def lane_block(q, size=lanes):
         return pl.ds(pl.multiple_of(q * size, 128), size)
@@ -1208,8 +942,7 @@
     gain_one = gain_all[...].astype(wide)[0:1]
     gain_two = gain_all[...].astype(wide)[1:2]
 
-    save(qkv_all, qkv_out)
-    save(gain_all, gain_out)
+    save_qkv = wires.fetch(wires.index(), qkv_all, qkv_kept)
 
     def norm_one(r):
         normed_one[r] = (scaled[r] * gain_one).astype(low)
@@ -1263,14 +996,9 @@
         lax.fori_loop(0, pairs, pair, 0)
         if g == 0:
             advance(g_out)
-    save(kv_all, kv_out)
-    save(q_rot, q_out)
-    save(mixed, mixed_out)
-    save(normed_one, normed_out)
     while g_out:
         advance(g_out)
     advance(g_unit)
-    save(out_all, out_out)
     pair_id = [wires.index() for _ in range(4)]
     for i in range(4):
         for j in range(2):
@@ -1290,7 +1018,6 @@
         nt[r] = (total * factor * gain_two).astype(low)
 
     by_rows(tokens, 16, norm_two)
-    save(hidden, hidden_out)
 
     gathers = []
     for source, target in ((nt, nt_all),):
@@ -1380,6 +1107,16 @@
         by_rows(tokens, 16, add)
         i = lax.rem(k - c + 4, 4)
         wires.copy(s_id + i, near.at[k, :, mine], came.at[i - 1], (t, k, d)).start()
+
+    padded = act_t.shape[0]
+    act = qkv_all.at[pl.ds(0, tokens * 8), pl.ds(0, padded)]
+    both = qkv_all.at[pl.ds(0, tokens * 8), pl.ds(padded, 2 * padded)]
+    both_t = qkv_all.at[pl.ds(tokens * 8, 2 * padded), pl.ds(0, tokens * 8)]
+    b_id = wires.index()
+
+    def stored(k):
+        where = pl.ds(pl.multiple_of(k * 2 * tokens, 16), 2 * tokens)
+        return pltpu.make_async_copy(stage_b, part_b.at[where], wires.recv.at[b_id])
 
     def swiglu(j, carry):
         stage_two(j)
@@ -1404,9 +1141,11 @@
                 + dot_nn(both[where, wide_units:], w3_all[1, :, piece])
             ).astype(low)
         wires.copy(n_id + k, part_rows(k, 1 - e), near.at[k], beside).start()
+        pl.when(j > 0)(lambda: stored(0).wait())
         for i in range(4):
             piece = slice(i * (width // 4), (i + 1) * (width // 4))
-            part_b[where, piece] = dot_nn(act[where], w3_all[2, :, piece]).astype(low)
+            stage_b[:, piece] = dot_nn(act[where], w3_all[2, :, piece]).astype(low)
+        stored(k).start()
         pl.when(j > 0)(lambda: stage_three(j - 1))
         pl.when(j > 2)(lambda: stage_four(j - 2))
         return carry
@@ -1415,8 +1154,10 @@
         stage_one(j)
     while g_unit:
         advance(g_unit)
+    save_qkv.wait()
+    wires.drain()
     lax.fori_loop(0, 4, swiglu, 0)
-    save(part_b, part_out)
+    stored(0).wait()
     stage_three(3)
     for k in range(4):
         away = c != k
@@ -1434,30 +1175,30 @@
     act_t[...] = act[...].T
     both_t[...] = both[...].T
 
-    def unit_grads(k, yy, place):
+    def unit_grads(k, yy):
         where = lane_block(k * 2 + yy, 256)
-        wide_units = act_t.shape[0]
         two = dot_nn(both_t[...], nt_all[:, where]).astype(low)
-        place[k, 0] = two[:units]
-        place[k, 1] = two[wide_units : wide_units + units]
-        place[k, 2] = dot_nn(act_t[...], gy_all[:, where]).astype(low)[:units]
+        w3_all[0, :units, where] = two[:units]
+        w3_all[1, :units, where] = two[padded : padded + units]
+        w3_all[2, :units, where] = dot_nn(act_t[...], gy_all[:, where]).astype(low)[:units]
 
     u_id = [wires.index() for _ in range(4)][0]
     across = (t, c, (1 - y) * 2 + e)
 
+    def half_grads(k):
+        return w3_all.at[:, pl.ds(0, units), lane_block(k * 2 + 1 - y, 256)]
+
     def send_units(k, carry):
-        unit_grads(k, 1 - y, unit_out)
-        wires.copy(u_id + k, unit_out.at[k], unit_in.at[k], across).start()
+        unit_grads(k, 1 - y)
+        wires.copy(u_id + k, half_grads(k), unit_in.at[k], across).start()
         return carry
 
     lax.fori_loop(0, 2, send_units, 0)
     stage_four(3)
     lax.fori_loop(2, 4, send_units, 0)
-    for k in range(4):
-        wires.owe(u_id + k, lambda k=k: unit_out.at[k])
 
     def keep_units(k, carry):
-        unit_grads(k, y, unit_own)
+        unit_grads(k, y)
         return carry
 
     lax.fori_loop(0, 2, keep_units, 0)
@@ -1475,89 +1216,289 @@
     last = wires.index()
     wires.push(last, lambda: gn_own.at[:, mine], lambda: gn_own.at[:, mine], over)
     lax.fori_loop(2, 4, keep_units, 0)
-    g_save = wires.index(), wires.index(), wires.index(), wires.index()
-    saves = []
+    wires.arrive(last, lambda: gn_own.at[:, other])
+    wires.drain()
     for k in range(4):
-        wires.arrive(u_id + k, lambda: unit_in.at[k])
-        for m in range(3):
-
-            def add(r):
-                both_y = unit_own[k, m, r].astype(wide) + unit_in[k, m, r].astype(wide)
-                unit_own[k, m, r] = both_y.astype(low)
-
-            by_rows(units, 16, add)
-        saves.append(wires.fetch(g_save[k], unit_own.at[k], g3.at[k]))
-    wires.arrive(last, lambda: gn_own.at[:, other])
-    saves.append(wires.fetch(wires.index(), gn_own, gn))
-    for copy in saves + kept_out:
-        copy.wait()
+        wires.owe(u_id + k, lambda k=k: half_grads(k))
+    for i, cond, device in (
+        (0, True, beside), (1, True, over), (2, c > 0, (t, c - 1, d)), (3, c < 3, (t, c + 1, d))
+    ):
+        only(
+            cond,
+            functools.partial(
+                pl.semaphore_signal, credit.at[i], inc=1, device_id=device, device_id_type=MESH
+            ),
+        )
+    load_qkv = wires.fetch(wires.index(), qkv_kept, qkv_all)
+    s_q, s_k, s_o = scratch[:4], scratch[4:8], scratch[8:12]
+    t_b = (
+        near, lambda k: part_g.at[pl.ds(k * tokens, tokens)], x_in, came.at[pl.ds(0, 4)], came.at[4]
+    )
+    g_unit = [unit_gather(wires, pos, w3_all, unit_in, u_id, g3_out)]
+    second = [token_scatter(wires, pos, part_b, branch, t_b, credit)]
+    mixed_t[...] = mixed[...].T
+    normed_t[...] = normed_one[...].T
+    gains_sum[...] = jnp.zeros_like(gains_sum)
+
+    def norm_two_back(r):
+        value, grad = norm_rows(gn_own[r].astype(wide), hidden[r], gain_two)
+        home = pl.ds(pl.multiple_of((c * 2 + e) * tokens + r.start, 16), 16)
+        total = gy_all[home].astype(wide) + value
+        grad_hidden[r] = total
+        grad_low[r] = total.astype(low)
+        gains_sum[1:2] += grad
+
+    by_rows(tokens, 16, norm_two_back)
+    advance(g_unit)
+
+    def out_grad(j, carry):
+        where = pl.ds(pl.multiple_of(j * 2 * lanes, 256), 2 * lanes)
+        nt_all[:, where] = dot_nn(mixed_t[...], grad_low[:, where]).astype(low)
+        return carry
+
+    lax.fori_loop(0, 8, out_grad, 0)
+    outs = [
+        plane_scatter(
+            wires, pos,
+            lambda k, yy: nt_all.at[:, lane_block(k * 4 + yy * 2 + 1 - e)],
+            lambda k, yy: nt_all.at[:, lane_block(k * 4 + yy * 2 + e)],
+            n_query, s_o, lambda r, v: go_out.__setitem__(r, v),
+        )
+    ]
+    advance(outs)
+
+    def mix_grad(j, carry):
+        where = pl.ds(pl.multiple_of(j * 256, 256), 256)
+        grad_mixed[:, where] = times_transposed(grad_low[...], out_all[where, :]).astype(low)
+        return carry
+
+    lax.fori_loop(0, n_query // 256, mix_grad, 0)
+    advance(outs, 4)
+    advance(second)
+    advance(g_unit)
+
+    scale = HEAD_SIZE ** (-0.5)
+    pairs = n_query // 256
+    for g in range(2):
+        keys = kv_all[:, g * HEAD_SIZE : (g + 1) * HEAD_SIZE]
+        values = kv_all[:, n_key + g * HEAD_SIZE : n_key + (g + 1) * HEAD_SIZE]
+        dk[...] = jnp.zeros_like(dk)
+        dv[...] = jnp.zeros_like(dv)
+
+        def pair(j, carry, g=g, keys=keys, values=values):
+            slab = pl.ds(pl.multiple_of((g * pairs + j) * 128, 128), 128)
+            q_two, m_two = q_rot[:, slab], grad_mixed[:, slab]
+            both = []
+            for h in range(2):
+                query = q_two[:, h * HEAD_SIZE : (h + 1) * HEAD_SIZE]
+                upstream = m_two[:, h * HEAD_SIZE : (h + 1) * HEAD_SIZE]
+                probs = head_probs(query, keys, allowed)
+                dprob = times_transposed(upstream, values)
+                delta = jnp.sum(probs * dprob, axis=-1, keepdims=True)
+                grad_scores = (probs * (dprob - delta)).astype(low)
+                both.append(dot_nn(grad_scores, keys))
+                dk[...] += transposed_times(grad_scores, query)
+                dv[...] += transposed_times(probs.astype(low), upstream)
+            grads = jnp.concatenate(both, axis=1) * scale
+            back = grads * cosine[...] - swap_halves(grads) * sine[...]
+            gqkv[:, slab] = back.astype(low)
+            return carry
+
+        lax.fori_loop(0, pairs, pair, 0)
+        for k in range(4):
+            block = slice(k * tokens, (k + 1) * tokens)
+            kv_part[k, :, g * HEAD_SIZE : (g + 1) * HEAD_SIZE] = (dk[block] * scale).astype(low)
+            kv_part[k, :, n_key + g * HEAD_SIZE : n_key + (g + 1) * HEAD_SIZE] = dv[block].astype(low)
+        advance(g_unit)
+        advance(second)
+
+    kvg_id = [wires.index() for _ in range(3)]
+    for i in range(3):
+        k = lax.rem(c + i + 1, 4)
+        wires.push(kvg_id[i], lambda k=k: kv_part.at[k], lambda i=i: kv_in.at[i], (t, k, d))
+
+    def q_grad(core, where):
+        for h, place in ((0, gy_all), (1, gq_part)):
+
+            def step(j, carry, h=h, place=place):
+                owner = j * 2 + core
+                here = lane_block(h * 8 + owner)
+                place[pl.ds(pl.multiple_of(owner * lanes, 16), lanes), where] = dot_nn(
+                    normed_t[here, :], gqkv[:, where]
+                ).astype(low)
+                return carry
+
+            lax.fori_loop(0, 4, step, 0)
+
+    def q_block(k, f, where):
+        place = gy_all if k < 2 else gq_part
+        return place.at[pl.ds(pl.multiple_of(((k % 2) * 4 + f) * lanes, 16), lanes), where]
+
+    def q_sums(where, scratches):
+        def done(r, value):
+            gq_out[r, where] = value
+
+        return plane_scatter(
+            wires, pos,
+            lambda k, yy: q_block(k, yy * 2 + 1 - e, where),
+            lambda k, yy: q_block(k, yy * 2 + e, where),
+            gq_out.shape[0], scratches, done,
+        )
+
+    first, rest = slice(0, n_query), slice(n_query, n_query + 2 * n_key)
+    q_grad(1 - e, first)
+    queries = [q_sums(first, s_q)]
+    advance(queries)
+    q_grad(e, first)
+    advance(queries, 4)
+    advance(g_unit)
+    total = kv_part[c].astype(wide)
+    for i in range(3):
+        wires.arrive(kvg_id[i], lambda: kv_in.at[i])
+        total = total + kv_in[i].astype(wide)
+    key_grads = total[:, :n_key]
+    key_grads = key_grads * cosine[...] - swap_halves(key_grads) * sine[...]
+    gqkv[:, n_query : n_query + n_key] = key_grads.astype(low)
+    gqkv[:, n_query + n_key :] = total[:, n_key:].astype(low)
+    q_grad(1 - e, rest)
+    others = [q_sums(rest, s_k)]
+    advance(others)
+    q_grad(e, rest)
+    load_qkv.wait()
+
+    def normed_grad(j, carry):
+        where = pl.ds(pl.multiple_of(j * 256, 256), 256)
+        pair_out[:, where] = times_transposed(gqkv[...], qkv_all[where, :]).astype(low)
+        return carry
+
+    lax.fori_loop(0, width // 256, normed_grad, 0)
+    p_id = wires.index()
+    wires.push(p_id, lambda: pair_out, lambda: pair_in, (1 - t, c, d))
+    advance(others, 4)
+    advance(g_unit)
+    wires.arrive(p_id, lambda: pair_in)
+
+    def norm_one_back(r):
+        upstream = pair_out[r].astype(wide) + pair_in[r].astype(wide)
+        value, grad = norm_rows(upstream, states[r].astype(wide), gain_one)
+        grad_states[r] = grad_hidden[r] + value
+        gains_sum[0:1] += grad
+
+    by_rows(tokens, 16, norm_one_back)
+    g_id = [wires.index() for _ in range(16)]
+
+    def gain_block(q):
+        return gains_sum.at[:, pl.ds(pl.multiple_of(q * lanes, 128), lanes)]
+
+    for i in range(1, 16):
+        q = lax.rem(me + i, 16)
+        wires.push(
+            g_id[i], lambda q=q: gain_block(q), lambda i=i: gain_in.at[i],
+            (t, q // 4, lax.rem(q, 4)),
+        )
+    while second or outs or queries or others:
+        advance(outs)
+        advance(queries)
+        advance(others)
+        advance(second)
+    while g_unit:
+        advance(g_unit)
+
+    def finish(r):
+        layer_out[r] = (hidden[r] + branch[r].astype(wide)).astype(low)
+
+    by_rows(tokens, 16, finish)
+    gain = gains_sum[:, pl.ds(pl.multiple_of(me * lanes, 128), lanes)]
+    for i in range(1, 16):
+        wires.arrive(g_id[i], lambda: gain_in.at[i])
+        gain = gain + gain_in[i]
+    gain_out[...] = gain
     wires.drain()
 
 
-def forward_call(lengths, states, gains, qkv, out_w, w3, gy, cosine, sine):
+def layer_call(lengths, states, gains, qkv, out_w, w3, gy, cosine, sine):
     shape = jax.ShapeDtypeStruct
     low, wide = jnp.bfloat16, jnp.float32
     tokens, width = states.shape
     n_query, lanes = out_w.shape
     n_all = qkv.shape[1]
+    n_rest = n_all - n_query
     units = w3.shape[1] // 8
     padded = -(-units // 128) * 128
-    all_tokens = tokens * 8
+    all_tokens, keys = tokens * 8, tokens * 4
     half = width // 2
     vm = pltpu.VMEM
     return pl.pallas_call(
-        forward_kernel,
-        name="forward",
+        layer_kernel,
+        name="layer",
         out_shape=(
+            shape((tokens, width), low),
+            shape((tokens, width), wide),
+            shape((3, units * 8, lanes), low),
+            shape((lanes, n_all), wide),
+            shape((n_query, lanes), wide),
+            shape((8, lanes), wide),
             shape((width, n_all), low),
-            shape((n_query, width), low),
-            shape((16, width), low),
-            shape((tokens, width), wide),
-            shape((tokens, width), low),
-            shape((tokens, n_query), low),
-            shape((tokens * 4, n_all - n_query), low),
-            shape((tokens, n_query), low),
             shape((all_tokens, width), low),
-            shape((4, 3, units, width // 8), low),
-            shape((tokens, width), low),
         ),
         in_specs=[pl.BlockSpec(memory_space=pltpu.MemorySpace.SMEM), pl.BlockSpec(memory_space=VMEM)]
         + [pl.BlockSpec(memory_space=HBM)] * 5
         + [pl.BlockSpec(memory_space=VMEM)] * 2,
-        out_specs=[pl.BlockSpec(memory_space=HBM)] * 11,
+        out_specs=[
+            pl.BlockSpec(memory_space=VMEM),
+            pl.BlockSpec(memory_space=VMEM),
+            pl.BlockSpec(memory_space=HBM),
+            pl.BlockSpec(memory_space=VMEM),
+            pl.BlockSpec(memory_space=VMEM),
+            pl.BlockSpec(memory_space=VMEM),
+            pl.BlockSpec(memory_space=HBM),
+            pl.BlockSpec(memory_space=HBM),
+        ],
         scratch_shapes=[
-            pltpu.SemaphoreType.DMA((200,)),
-            pltpu.SemaphoreType.DMA((200,)),
+            pltpu.SemaphoreType.DMA((320,)),
+            pltpu.SemaphoreType.DMA((320,)),
+            pltpu.SemaphoreType.REGULAR((4,)),
             vm((width, n_all), low),
             vm((n_query, width), low),
             vm((16, width), low),
             vm((tokens, width), wide),
             vm((tokens, width), low),
             vm((tokens, n_query), low),
-            vm((tokens * 4, n_all - n_query), low),
+            vm((keys, n_rest), low),
             vm((tokens, n_query), low),
-            vm((all_tokens, width), low),
             vm((tokens, width), low),
-            vm((4, 3, units, width // 8), low),
-            vm((4, 3, units, width // 8), low),
-            vm((4, 3, units, width // 8), low),
-            vm((tokens, width), wide),
             vm((3, padded, width), low),
             vm((all_tokens, width), low),
             vm((all_tokens, width), low),
-            vm((all_tokens, padded), low),
-            vm((all_tokens, 2 * padded), low),
             vm((padded, all_tokens), low),
-            vm((2 * padded, all_tokens), low),
             vm((all_tokens, width), low),
-            vm((tokens, n_all - n_query), low),
+            vm((2 * tokens, width), low),
+            vm((4, 3, units, width // 8), low),
+            vm((tokens, n_rest), low),
             vm((tokens, width), low),
             vm((tokens, width), low),
             vm((tokens, width), low),
             vm((4, tokens, width), low),
             vm((4, tokens, half), low),
-            vm((3, tokens, half), low),
-        ],
+            vm((5, tokens, half), low),
+            vm((tokens, width), wide),
+            vm((tokens, width), low),
+            vm((tokens, width), low),
+            vm((n_query, tokens), low),
+            vm((tokens, n_query), low),
+            vm((tokens, n_all), low),
+            vm((width, tokens), low),
+            vm((8 * lanes, n_all), low),
+            vm((keys, HEAD_SIZE), wide),
+            vm((keys, HEAD_SIZE), wide),
+            vm((4, tokens, n_rest), low),
+            vm((3, tokens, n_rest), low),
+            vm((8, width), wide),
+            vm((16, 8, lanes), wide),
+        ]
+        + plane_scratch((lanes, n_query))
+        + plane_scratch((lanes, n_rest))
+        + plane_scratch((n_query, lanes)),
         compiler_params=pltpu.CompilerParams(
             collective_id=1, has_side_effects=True, vmem_limit_bytes=63 << 20
         ),
@@ -1585,12 +1526,8 @@
         [first_gain[None], second_gain[None], jnp.zeros((14, lanes), low)], axis=0
     )
     w3 = jnp.stack([w_gate.T, w_up.T, w_down])
-    qkv_all, out_all, gain_all, hidden, normed_one, q_rot, kv_all, mixed, part_b, g3, gn = (
-        forward_call(lengths, states[0], gains, qkv, w_out, w3, grad_y, cosine, sine)
-    )
-    layer_out, grad_states, g3, gq, go, gain = backward_call(
-        lengths, gn, part_b, g3, qkv_all, out_all, gain_all, hidden, states[0], grad_y,
-        normed_one, q_rot, kv_all, mixed, cosine, sine,
+    layer_out, grad_states, g3, gq, go, gain, _, _ = layer_call(
+        lengths, states[0], gains, qkv, w_out, w3, grad_y, cosine, sine
     )
     return (
         layer_out[None],

time: 394 us -> 375 us (0.952)
  Pallas kernels: 369 us -> 351 us
    pallas_call x2 -> x1, Pallas kernels: 369 us -> 351 us  [layer_call(): pl.pallas_call(layer_kernel, name='layer', out_shape=(shape((tokens, widt...]
where the time goes in v2:
time: 375 us
  Pallas kernels  351 us (94%)
  local copies, waits for them, and re-layouts  11.9 us (3%)
  other arithmetic  10.4 us (3%)
    pallas_call x1, Pallas kernels, layer_call(): pl.pallas_call(layer_kernel, name='layer', out_shape=(shape((tokens, widt...  351 us

profile of v2, /device:TPU:8, one launch (start us, length us, event | category | flops | bytes accessed | tf_op | source)
XLA Modules:
  0.0 374.7 jit_solution(9289356492751068990)
XLA Ops:
  0.6 0.0 copy-start.2
  0.7 0.0 copy-start.1
  1.5 0.1 pad.8.clone
  1.5 1.3 maximum_maximum_fusion.gains
  2.9 0.1 multiply_sine_fusion
  3.0 0.1 copy.29
  3.1 0.6 broadcast_multiply_fusion.sine
  3.8 0.7 copy.30.cosine
  4.5 0.0 copy-start.3
  4.5 1.8 pad_maximum_fusion.1.qkv
  6.3 1.9 bitcast_select_fusion.gy
  8.3 0.0 copy-done.1
  8.3 0.3 copy.27
  8.6 0.0 copy-done.2
  8.6 0.3 copy.28
  9.0 0.0 copy-done.3
  9.0 1.6 pad_maximum_fusion.w3
  10.6 350.9 %layer.1 = (bf16[128,2048]{1,0:T(8,128)(2,1)}, f32[128,2048]{1,0:T(8,128)}, bf16[3,2816,128]{2,1,0:T(8,128)(2,1)}, f32[128,1280]{1,0:T(8,128)}, f32[1024,128]{1,...) custom-call(s32[1]{0:T(128)} %copy.36.lengths, bf16[128,2048]{1,0:T(8,128)(2,1)} %bitcast.39, ...), custom_call_target="tpu_custom_call" | custom-call | tf_op jit(solution)/shard_map/layer/pallas_call | solution.py:1431
  361.4 1.3 slice_bitcast_fusion
  362.7 1.5 fusion.2
  364.2 1.9 slice.25
  366.1 2.9 bitcast_convert_fusion
  369.0 1.5 copy.32
  370.6 0.0 copy-start.5
  370.6 0.0 copy-start
  370.6 1.5 copy.31
  372.1 0.0 copy-done.5
  372.1 0.8 copy.37
  372.9 0.0 copy-done
  372.9 1.0 copy.38
  373.9 0.0 copy-done.4
  373.9 0.8 copy.39
  (8 shorter events, 0.0 us)
Async XLA Ops:
  0.6 8.0 %copy-start.2 = (bf16[128,2816]{1,0:T(8,128)(2,1)S(1)}, bf16[128,2816]{1,0:T(8,128)(2,1)}, u32[]{:S(2)}) copy-start(bf16[128,2816]{1,0:T(8,128)(2,1)} %param.21) | copy-start | bytes 2162692
  0.7 7.6 %copy-start.1 = (bf16[128,2816]{1,0:T(8,128)(2,1)S(1)}, bf16[128,2816]{1,0:T(8,128)(2,1)}, u32[]{:S(2)}) copy-start(bf16[128,2816]{1,0:T(8,128)(2,1)} %param.20) | copy-start | bytes 2162692
  4.5 4.5 %copy-start.3 = (bf16[2816,128]{1,0:T(8,128)(2,1)S(1)}, bf16[2816,128]{1,0:T(8,128)(2,1)}, u32[]{:S(2)}) copy-start(bf16[2816,128]{1,0:T(8,128)(2,1)} %param.22) | copy-start | bytes 2162692
  370.6 1.5 copy-start.5
  370.6 2.3 copy-start
  372.1 1.8 copy-start.4

commit v3 on v2

--- a/solution.py
+++ b/solution.py
@@ -584,7 +584,11 @@
     return lax.dot_general(a, b, (((1,), (0,)), ((), ())), preferred_element_type=jnp.float32)
 
 
-def by_rows(count, step, act):
+def by_rows(count, width, act):
+    step = max(16, 32768 // width)
+    while count % step:
+        step -= 16
+
     def body(i, carry):
         act(pl.ds(pl.multiple_of(i * step, step), step))
         return carry
@@ -602,30 +606,32 @@
     r_id = [wires.index() for _ in range(4)]
     l_id = [wires.index() for _ in range(4)]
 
-    def hop(k):
-        place = keep(k)
-        for go, edge, number, way in ((c < k, 0, r_id[k], 1), (c > k, 3, l_id[k], -1)):
-            if (k == 0 and way > 0) or (k == 3 and way < 0):
-                continue
-            wires.arrive(number, lambda: came.at[k], go & (c != edge))
-
-            def act():
-                def first(r):
-                    place[r] = value(k, r).astype(place.dtype)
-
-                def later(r):
-                    place[r] = (value(k, r) + came[k, r].astype(wide)).astype(place.dtype)
-
-                pl.when(c == edge)(lambda: by_rows(height, 16, first))
-                pl.when(c != edge)(lambda: by_rows(height, 16, later))
-
-            pl.when(go)(act)
-            target = (t, c + way, d)
-            if way > 0:
-                wires.push(number, lambda: keep(k), lambda: came.at[k], target, go)
-            else:
-                wires.push(number, lambda: keep(k), lambda: extra, target, go & (c == k + 1))
-                wires.push(number, lambda: keep(k), lambda: came.at[k], target, go & (c > k + 1))
+    def stage(s):
+        for edge, way, blocks, number in (
+            (s, 1, range(3, s, -1), r_id), (3 - s, -1, range(0, 3 - s), l_id)
+        ):
+            here = c == edge
+            for k in blocks:
+
+                def act(k=k, number=number):
+                    place = keep(k)
+                    if s > 0:
+                        wires.arrive(number[k], lambda: came.at[k])
+
+                    def add(r):
+                        total = value(k, r)
+                        if s > 0:
+                            total = total + came[k, r].astype(wide)
+                        place[r] = total.astype(place.dtype)
+
+                    by_rows(height, extra.shape[-1], add)
+
+                pl.when(here)(act)
+                target = extra if way < 0 and k == edge - 1 else came.at[k]
+                wires.push(
+                    number[k], lambda k=k: keep(k), lambda target=target: target,
+                    (t, c + way, d), here,
+                )
 
     def finish():
         for k in range(4):
@@ -644,11 +650,11 @@
                         total = total + extra[r].astype(wide)
                     done(r, total)
 
-                by_rows(height, 16, add)
+                by_rows(height, extra.shape[-1], add)
 
             pl.when(c == k)(act)
 
-    return hop, finish
+    return stage, finish
 
 
 def token_scatter(wires, pos, part, out, scratch, credit):
@@ -685,7 +691,7 @@
             total = own(k)[r, other].astype(wide) + near[k, r, other].astype(wide)
             near[k, r, other] = total.astype(near.dtype)
 
-        by_rows(tokens, 16, away)
+        by_rows(tokens, half, away)
         wires.push(
             x_id[k], lambda k=k: near.at[k, :, other], lambda k=k: x_in.at[k], (1 - t, c, y * 2 + e)
         )
@@ -701,14 +707,15 @@
     def done(r, total):
         out[r, mine] = total.astype(out.dtype)
 
-    hop, finish = chain_sum(
+    stage, finish = chain_sum(
         wires, pos, tokens, value, lambda k: near.at[k, :, mine], came, extra, done
     )
     pl.when(c < 3)(lambda: pl.semaphore_wait(credit.at[2], 1))
     pl.when(c > 0)(lambda: pl.semaphore_wait(credit.at[3], 1))
     for k in ORDER:
         wires.arrive(x_id[k], lambda: x_in.at[k])
-        hop(k)
+    for s in range(3):
+        stage(s)
         yield
     finish()
     wires.push(last, lambda: out.at[:, mine], lambda: out.at[:, mine], (1 - t, c, y * 2 + e))
@@ -716,12 +723,12 @@
     wires.arrive(last, lambda: out.at[:, other])
 
 
-def plane_scatter(wires, pos, out_block, own_block, height, scratch, done):
+def plane_scatter(wires, pos, out_block, own_block, height, scratch, done, straight=False):
     t, c, y, e = pos
     near, y_in, came, extra = scratch
     wide = jnp.float32
     d_y, d_e = (1 - y) * 2 + e, y * 2 + 1 - e
-    e_id = {(k, f): wires.index() for k in range(4) for f in range(2)}
+    e_id = {(k, f): wires.index() for f in range(2) for k in range(4)}
     y_id = [wires.index() for _ in range(4)]
     for f in range(2):
         yy = (1 - y) if f == 0 else y
@@ -739,9 +746,17 @@
             total = block[r].astype(wide) + near[k, r].astype(wide)
             near[k, r] = total.astype(near.dtype)
 
-        by_rows(height, 16, away)
+        by_rows(height, extra.shape[-1], away)
         wires.push(y_id[k], lambda k=k: near.at[k], lambda k=k: y_in.at[k], (t, c, d_y))
         yield
+
+    def block_value(k, r):
+        block = own_block(k, y)
+        return (
+            block[r].astype(wide)
+            + near[4 + k, r].astype(wide)
+            + y_in[k, r].astype(wide)
+        )
 
     def value(k, r):
         return (
@@ -750,13 +765,44 @@
             + y_in[k, r].astype(wide)
         )
 
-    hop, finish = chain_sum(
+    if straight:
+        s_id = [wires.index() for _ in range(4)]
+        for far in (3, 1, 2):
+            k = lax.rem(c + far, 4)
+            wires.arrive(e_id[0, 1] + k, lambda: near.at[4 + k])
+            wires.arrive(y_id[0] + k, lambda: y_in.at[k])
+
+            def settle(r):
+                near[4 + k, r] = block_value(k, r).astype(near.dtype)
+
+            by_rows(height, extra.shape[-1], settle)
+            wires.push(
+                s_id[far], lambda k=k: near.at[4 + k], lambda far=far: came.at[far],
+                (t, k, y * 2 + e),
+            )
+            yield
+        wires.arrive(e_id[0, 1] + c, lambda: near.at[4 + c])
+        wires.arrive(y_id[0] + c, lambda: y_in.at[c])
+        for far in (3, 1, 2):
+            wires.arrive(s_id[far], lambda: came.at[far])
+
+        def add(r):
+            total = block_value(c, r)
+            for far in (1, 2, 3):
+                total = total + came[far, r].astype(wide)
+            done(r, total)
+
+        by_rows(height, extra.shape[-1], add)
+        return
+
+    stage, finish = chain_sum(
         wires, pos, height, value, lambda k: near.at[4 + k], came, extra, done
     )
     for k in ORDER:
         wires.arrive(e_id[k, 1], lambda: near.at[4 + k])
         wires.arrive(y_id[k], lambda: y_in.at[k])
-        hop(k)
+    for s in range(3):
+        stage(s)
         yield
     finish()
 
@@ -789,7 +835,7 @@
                 both = grads[m, r, where].astype(wide) + came[k, m, r].astype(wide)
                 grads[m, r, where] = both.astype(grads.dtype)
 
-            by_rows(units, 16, add)
+            by_rows(units, 2 * lanes, add)
         for f in range(2):
             g = e if f == 0 else 1 - e
             src = lambda k=k, g=g: grads.at[
@@ -923,7 +969,7 @@
         x = states[r].astype(wide)
         scaled[r] = x * lax.rsqrt(jnp.mean(x * x, axis=-1, keepdims=True) + EPS)
 
-    by_rows(tokens, 16, scale_rows)
+    by_rows(tokens, width, scale_rows)
     advance(g_qkv)
     advance(g_out)
     advance(g_gy)
@@ -947,7 +993,7 @@
     def norm_one(r):
         normed_one[r] = (scaled[r] * gain_one).astype(low)
 
-    by_rows(tokens, 16, norm_one)
+    by_rows(tokens, width, norm_one)
 
     def turned(x):
         return x * cosine[...] + swap_halves(x) * sine[...]
@@ -1017,7 +1063,7 @@
         factor = lax.rsqrt(jnp.mean(total * total, axis=-1, keepdims=True) + EPS)
         nt[r] = (total * factor * gain_two).astype(low)
 
-    by_rows(tokens, 16, norm_two)
+    by_rows(tokens, width, norm_two)
 
     gathers = []
     for source, target in ((nt, nt_all),):
@@ -1085,7 +1131,7 @@
             total = ours[r, other].astype(wide) + near[k, r, other].astype(wide)
             near[k, r, other] = total.astype(low)
 
-        by_rows(tokens, 16, away)
+        by_rows(tokens, half, away)
         wires.copy(r_id + k, near.at[k, :, other], x_in.at[k], over).start()
 
     def kept(k, r):
@@ -1104,7 +1150,7 @@
         def add(r):
             near[k, r, mine] = kept(k, r).astype(low)
 
-        by_rows(tokens, 16, add)
+        by_rows(tokens, half, add)
         i = lax.rem(k - c + 4, 4)
         wires.copy(s_id + i, near.at[k, :, mine], came.at[i - 1], (t, k, d)).start()
 
@@ -1188,7 +1234,8 @@
     def half_grads(k):
         return w3_all.at[:, pl.ds(0, units), lane_block(k * 2 + 1 - y, 256)]
 
-    def send_units(k, carry):
+    def send_units(j, carry):
+        k = lax.rem(c + 1 + j, 4)
         unit_grads(k, 1 - y)
         wires.copy(u_id + k, half_grads(k), unit_in.at[k], across).start()
         return carry
@@ -1197,11 +1244,16 @@
     stage_four(3)
     lax.fori_loop(2, 4, send_units, 0)
 
-    def keep_units(k, carry):
-        unit_grads(k, y)
+    def keep_units(j, carry):
+        unit_grads(lax.rem(c + 1 + j, 4), y)
         return carry
 
     lax.fori_loop(0, 2, keep_units, 0)
+    g_unit = [unit_gather(wires, pos, w3_all, unit_in, u_id, g3_out)]
+    owed, bulk = wires.sent, []
+    wires.sent = bulk
+    advance(g_unit)
+    wires.sent = owed
     wires.arrive(r_id + c, lambda: x_in.at[c])
     for i in (3, 1, 2):
         wires.arrive(s_id + i, lambda: came.at[i - 1])
@@ -1212,12 +1264,17 @@
             total = total + came[i, r].astype(wide)
         gn_own[r, mine] = total.astype(low)
 
-    by_rows(tokens, 16, done)
+    by_rows(tokens, half, done)
     last = wires.index()
     wires.push(last, lambda: gn_own.at[:, mine], lambda: gn_own.at[:, mine], over)
     lax.fori_loop(2, 4, keep_units, 0)
+    wires.sent = bulk
+    advance(g_unit)
+    wires.sent = owed
     wires.arrive(last, lambda: gn_own.at[:, other])
+    wires.sent = owed
     wires.drain()
+    wires.sent = bulk
     for k in range(4):
         wires.owe(u_id + k, lambda k=k: half_grads(k))
     for i, cond, device in (
@@ -1234,8 +1291,8 @@
     t_b = (
         near, lambda k: part_g.at[pl.ds(k * tokens, tokens)], x_in, came.at[pl.ds(0, 4)], came.at[4]
     )
-    g_unit = [unit_gather(wires, pos, w3_all, unit_in, u_id, g3_out)]
     second = [token_scatter(wires, pos, part_b, branch, t_b, credit)]
+    advance(second)
     mixed_t[...] = mixed[...].T
     normed_t[...] = normed_one[...].T
     gains_sum[...] = jnp.zeros_like(gains_sum)
@@ -1248,8 +1305,8 @@
         grad_low[r] = total.astype(low)
         gains_sum[1:2] += grad
 
-    by_rows(tokens, 16, norm_two_back)
-    advance(g_unit)
+    by_rows(tokens, width, norm_two_back)
+    advance(second)
 
     def out_grad(j, carry):
         where = pl.ds(pl.multiple_of(j * 2 * lanes, 256), 2 * lanes)
@@ -1274,7 +1331,6 @@
 
     lax.fori_loop(0, n_query // 256, mix_grad, 0)
     advance(outs, 4)
-    advance(second)
     advance(g_unit)
 
     scale = HEAD_SIZE ** (-0.5)
@@ -1309,30 +1365,21 @@
             block = slice(k * tokens, (k + 1) * tokens)
             kv_part[k, :, g * HEAD_SIZE : (g + 1) * HEAD_SIZE] = (dk[block] * scale).astype(low)
             kv_part[k, :, n_key + g * HEAD_SIZE : n_key + (g + 1) * HEAD_SIZE] = dv[block].astype(low)
-        advance(g_unit)
-        advance(second)
-
     kvg_id = [wires.index() for _ in range(3)]
     for i in range(3):
         k = lax.rem(c + i + 1, 4)
         wires.push(kvg_id[i], lambda k=k: kv_part.at[k], lambda i=i: kv_in.at[i], (t, k, d))
 
-    def q_grad(core, where):
-        for h, place in ((0, gy_all), (1, gq_part)):
-
-            def step(j, carry, h=h, place=place):
-                owner = j * 2 + core
-                here = lane_block(h * 8 + owner)
-                place[pl.ds(pl.multiple_of(owner * lanes, 16), lanes), where] = dot_nn(
-                    normed_t[here, :], gqkv[:, where]
-                ).astype(low)
-                return carry
-
-            lax.fori_loop(0, 4, step, 0)
-
-    def q_block(k, f, where):
-        place = gy_all if k < 2 else gq_part
-        return place.at[pl.ds(pl.multiple_of(((k % 2) * 4 + f) * lanes, 16), lanes), where]
+    def q_block(place, i, where):
+        return place.at[pl.ds(pl.multiple_of(i * lanes, 16), lanes), where]
+
+    def q_grad(core, place, where):
+        def step(i, carry):
+            here = lane_block(i * 2 + core)
+            q_block(place, i, where)[...] = dot_nn(normed_t[here, :], gqkv[:, where]).astype(low)
+            return carry
+
+        lax.fori_loop(0, 8, step, 0)
 
     def q_sums(where, scratches):
         def done(r, value):
@@ -1340,17 +1387,18 @@
 
         return plane_scatter(
             wires, pos,
-            lambda k, yy: q_block(k, yy * 2 + 1 - e, where),
-            lambda k, yy: q_block(k, yy * 2 + e, where),
+            lambda k, yy: q_block(gy_all, k * 2 + yy, where),
+            lambda k, yy: q_block(gq_part, k * 2 + yy, where),
             gq_out.shape[0], scratches, done,
         )
 
     first, rest = slice(0, n_query), slice(n_query, n_query + 2 * n_key)
-    q_grad(1 - e, first)
+    q_grad(1 - e, gy_all, first)
     queries = [q_sums(first, s_q)]
     advance(queries)
-    q_grad(e, first)
+    q_grad(e, gq_part, first)
     advance(queries, 4)
+    advance(second)
     advance(g_unit)
     total = kv_part[c].astype(wide)
     for i in range(3):
@@ -1360,10 +1408,10 @@
     key_grads = key_grads * cosine[...] - swap_halves(key_grads) * sine[...]
     gqkv[:, n_query : n_query + n_key] = key_grads.astype(low)
     gqkv[:, n_query + n_key :] = total[:, n_key:].astype(low)
-    q_grad(1 - e, rest)
+    q_grad(1 - e, gy_all, rest)
     others = [q_sums(rest, s_k)]
     advance(others)
-    q_grad(e, rest)
+    q_grad(e, gq_part, rest)
     load_qkv.wait()
 
     def normed_grad(j, carry):
@@ -1375,7 +1423,9 @@
     p_id = wires.index()
     wires.push(p_id, lambda: pair_out, lambda: pair_in, (1 - t, c, d))
     advance(others, 4)
-    advance(g_unit)
+    advance(second)
+    advance(outs)
+    advance(second)
     wires.arrive(p_id, lambda: pair_in)
 
     def norm_one_back(r):
@@ -1384,7 +1434,7 @@
         grad_states[r] = grad_hidden[r] + value
         gains_sum[0:1] += grad
 
-    by_rows(tokens, 16, norm_one_back)
+    by_rows(tokens, width, norm_one_back)
     g_id = [wires.index() for _ in range(16)]
 
     def gain_block(q):
@@ -1396,18 +1446,26 @@
             g_id[i], lambda q=q: gain_block(q), lambda i=i: gain_in.at[i],
             (t, q // 4, lax.rem(q, 4)),
         )
-    while second or outs or queries or others:
-        advance(outs)
-        advance(queries)
-        advance(others)
-        advance(second)
+    advance(outs)
+    advance(second)
+    advance(others)
+    advance(outs)
+    advance(queries)
+    advance(others)
+    advance(outs)
+    advance(queries)
+    advance(others)
+    advance(queries)
+    advance(others)
+    advance(queries)
+    advance(second)
     while g_unit:
         advance(g_unit)
 
     def finish(r):
         layer_out[r] = (hidden[r] + branch[r].astype(wide)).astype(low)
 
-    by_rows(tokens, 16, finish)
+    by_rows(tokens, width, finish)
     gain = gains_sum[:, pl.ds(pl.multiple_of(me * lanes, 128), lanes)]
     for i in range(1, 16):
         wires.arrive(g_id[i], lambda: gain_in.at[i])

time: 375 us -> 336 us (0.90)
  Pallas kernels: 351 us -> 308 us
    pallas_call x1, Pallas kernels: 351 us -> 308 us  [layer_call(): pl.pallas_call(layer_kernel, name='layer', out_shape=(shape((tokens, widt...]
where the time goes in v3:
time: 336 us; the launch traced here: 332 us
  Pallas kernels  308 us (92%)
  local copies, waits for them, and re-layouts  11.9 us (4%)
  other arithmetic  10.4 us (3%)
    pallas_call x1, Pallas kernels, layer_call(): pl.pallas_call(layer_kernel, name='layer', out_shape=(shape((tokens, widt...  308 us

profile of v3, /device:TPU:8, one launch (start us, length us, event | category | flops | bytes accessed | tf_op | source)
XLA Modules:
  0.0 332.0 jit_solution(2592667922676488056)
XLA Ops:
  0.6 0.0 copy-start.2
  0.7 0.0 copy-start.1
  1.5 0.1 pad.8.clone
  1.5 1.3 maximum_maximum_fusion.gains
  2.9 0.1 multiply_sine_fusion
  3.0 0.1 copy.29
  3.1 0.6 broadcast_multiply_fusion.sine
  3.8 0.7 copy.30.cosine
  4.5 0.0 copy-start.3
  4.5 1.8 pad_maximum_fusion.1.qkv
  6.3 1.9 bitcast_select_fusion.gy
  8.3 0.0 copy-done.1
  8.3 0.3 copy.27
  8.6 0.0 copy-done.2
  8.6 0.3 copy.28
  9.0 0.0 copy-done.3
  9.0 1.6 pad_maximum_fusion.w3
  10.6 308.2 %layer.1 = (bf16[128,2048]{1,0:T(8,128)(2,1)}, f32[128,2048]{1,0:T(8,128)}, bf16[3,2816,128]{2,1,0:T(8,128)(2,1)}, f32[128,1280]{1,0:T(8,128)}, f32[1024,128]{1,...) custom-call(s32[1]{0:T(128)} %copy.36.lengths, bf16[128,2048]{1,0:T(8,128)(2,1)} %bitcast.39, ...), custom_call_target="tpu_custom_call" | custom-call | tf_op jit(solution)/shard_map/layer/pallas_call | solution.py:1489
  318.7 1.3 slice_bitcast_fusion
  320.0 1.5 fusion.2
  321.5 1.9 slice.25
  323.4 2.9 bitcast_convert_fusion
  326.3 1.5 copy.32
  327.9 0.0 copy-start.5
  327.9 0.0 copy-start
  327.9 1.5 copy.31
  329.4 0.0 copy-done.5
  329.4 0.8 copy.37
  330.2 0.0 copy-done
  330.2 1.0 copy.38
  331.2 0.0 copy-done.4
  331.2 0.8 copy.39
  (8 shorter events, 0.0 us)
Async XLA Ops:
  0.6 8.0 %copy-start.2 = (bf16[128,2816]{1,0:T(8,128)(2,1)S(1)}, bf16[128,2816]{1,0:T(8,128)(2,1)}, u32[]{:S(2)}) copy-start(bf16[128,2816]{1,0:T(8,128)(2,1)} %param.21) | copy-start | bytes 2162692
  0.7 7.6 %copy-start.1 = (bf16[128,2816]{1,0:T(8,128)(2,1)S(1)}, bf16[128,2816]{1,0:T(8,128)(2,1)}, u32[]{:S(2)}) copy-start(bf16[128,2816]{1,0:T(8,128)(2,1)} %param.20) | copy-start | bytes 2162692
  4.5 4.5 %copy-start.3 = (bf16[2816,128]{1,0:T(8,128)(2,1)S(1)}, bf16[2816,128]{1,0:T(8,128)(2,1)}, u32[]{:S(2)}) copy-start(bf16[2816,128]{1,0:T(8,128)(2,1)} %param.22) | copy-start | bytes 2162692
  327.9 1.5 copy-start.5
  327.9 2.3 copy-start
  329.4 1.8 copy-start.4

commit v4 on v3

--- a/solution.py
+++ b/solution.py
@@ -825,7 +825,7 @@
     o_id = [wires.index() for _ in range(8)]
     here = pl.ds(pl.multiple_of(me * units, 16), units)
     fetch = []
-    for far in (1, 2, 3, 0):
+    for far in (2, 1, 3, 0):
         k = lax.rem(c + far, 4)
         wires.arrive(y_id + k, lambda: came.at[k])
         where = pl.ds(pl.multiple_of((k * 2 + y) * 2 * lanes, 256), 2 * lanes)
@@ -1235,7 +1235,7 @@
         return w3_all.at[:, pl.ds(0, units), lane_block(k * 2 + 1 - y, 256)]
 
     def send_units(j, carry):
-        k = lax.rem(c + 1 + j, 4)
+        k = lax.rem(c + pick(j, (2, 1, 3, 0)), 4)
         unit_grads(k, 1 - y)
         wires.copy(u_id + k, half_grads(k), unit_in.at[k], across).start()
         return carry
@@ -1245,7 +1245,7 @@
     lax.fori_loop(2, 4, send_units, 0)
 
     def keep_units(j, carry):
-        unit_grads(lax.rem(c + 1 + j, 4), y)
+        unit_grads(lax.rem(c + pick(j, (2, 1, 3, 0)), 4), y)
         return carry
 
     lax.fori_loop(0, 2, keep_units, 0)

time: 336 us -> 325 us (0.967)
  Pallas kernels: 308 us -> 299 us
    pallas_call x1, Pallas kernels: 308 us -> 299 us  [layer_call(): pl.pallas_call(layer_kernel, name='layer', out_shape=(shape((tokens, widt...]
where the time goes in v4:
time: 325 us; the launch traced here: 323 us
  Pallas kernels  299 us (92%)
  local copies, waits for them, and re-layouts  11.9 us (4%)
  other arithmetic  10.4 us (3%)
    pallas_call x1, Pallas kernels, layer_call(): pl.pallas_call(layer_kernel, name='layer', out_shape=(shape((tokens, widt...  299 us

profile of v4, /device:TPU:8, one launch (start us, length us, event | category | flops | bytes accessed | tf_op | source)
XLA Modules:
  0.0 322.5 jit_solution(8411586672287816725)
XLA Ops:
  0.6 0.0 copy-start.2
  0.7 0.0 copy-start.1
  1.5 0.1 pad.8.clone
  1.5 1.3 maximum_maximum_fusion.gains
  2.9 0.1 multiply_sine_fusion
  3.0 0.1 copy.29
  3.1 0.6 broadcast_multiply_fusion.sine
  3.8 0.7 copy.30.cosine
  4.5 0.0 copy-start.3
  4.5 1.8 pad_maximum_fusion.1.qkv
  6.3 1.9 bitcast_select_fusion.gy
  8.3 0.0 copy-done.1
  8.3 0.3 copy.27
  8.6 0.0 copy-done.2
  8.6 0.3 copy.28
  9.0 0.0 copy-done.3
  9.0 1.6 pad_maximum_fusion.w3
  10.6 298.7 %layer.1 = (bf16[128,2048]{1,0:T(8,128)(2,1)}, f32[128,2048]{1,0:T(8,128)}, bf16[3,2816,128]{2,1,0:T(8,128)(2,1)}, f32[128,1280]{1,0:T(8,128)}, f32[1024,128]{1,...) custom-call(s32[1]{0:T(128)} %copy.36.lengths, bf16[128,2048]{1,0:T(8,128)(2,1)} %bitcast.39, ...), custom_call_target="tpu_custom_call" | custom-call | tf_op jit(solution)/shard_map/layer/pallas_call | solution.py:1489
  309.3 1.3 slice_bitcast_fusion
  310.6 1.5 fusion.2
  312.1 1.9 slice.25
  314.0 2.9 bitcast_convert_fusion
  316.9 1.5 copy.32
  318.4 0.0 copy-start.5
  318.4 0.0 copy-start
  318.4 1.5 copy.31
  320.0 0.0 copy-done.5
  320.0 0.8 copy.37
  320.8 0.0 copy-done
  320.8 1.0 copy.38
  321.8 0.0 copy-done.4
  321.8 0.8 copy.39
  (8 shorter events, 0.0 us)
Async XLA Ops:
  0.6 8.0 %copy-start.2 = (bf16[128,2816]{1,0:T(8,128)(2,1)S(1)}, bf16[128,2816]{1,0:T(8,128)(2,1)}, u32[]{:S(2)}) copy-start(bf16[128,2816]{1,0:T(8,128)(2,1)} %param.21) | copy-start | bytes 2162692
  0.7 7.6 %copy-start.1 = (bf16[128,2816]{1,0:T(8,128)(2,1)S(1)}, bf16[128,2816]{1,0:T(8,128)(2,1)}, u32[]{:S(2)}) copy-start(bf16[128,2816]{1,0:T(8,128)(2,1)} %param.20) | copy-start | bytes 2162692
  4.5 4.5 %copy-start.3 = (bf16[2816,128]{1,0:T(8,128)(2,1)S(1)}, bf16[2816,128]{1,0:T(8,128)(2,1)}, u32[]{:S(2)}) copy-start(bf16[2816,128]{1,0:T(8,128)(2,1)} %param.22) | copy-start | bytes 2162692
  318.4 1.5 copy-start.5
  318.4 2.3 copy-start
  320.0 1.8 copy-start.4

commit v5 on v4

--- a/solution.py
+++ b/solution.py
@@ -825,7 +825,7 @@
     o_id = [wires.index() for _ in range(8)]
     here = pl.ds(pl.multiple_of(me * units, 16), units)
     fetch = []
-    for far in (2, 1, 3, 0):
+    for far in (2, 3, 1, 0):
         k = lax.rem(c + far, 4)
         wires.arrive(y_id + k, lambda: came.at[k])
         where = pl.ds(pl.multiple_of((k * 2 + y) * 2 * lanes, 256), 2 * lanes)
@@ -901,7 +901,7 @@
 
 def layer_kernel(
     lengths, states, gains, qkv, out_w, w3, gy, cosine, sine,
-    layer_out, grad_states, g3_out, gq_out, go_out, gain_out, qkv_kept, part_b,
+    layer_out, grad_states, g3_out, gq_out, gk_out, gv_out, go_out, gain_out, qkv_kept, part_b,
     send, recv, credit, qkv_all, out_all, gain_all, hidden, normed_one, q_rot, kv_all, mixed, gn_own,
     w3_all, gy_all, nt_all, act_t, part_g, stage_b, unit_in, kv_own, pair_out, pair_in, nt,
     near, x_in, came, grad_hidden, grad_low, branch, mixed_t, grad_mixed, gqkv, normed_t, gq_part,
@@ -1235,7 +1235,7 @@
         return w3_all.at[:, pl.ds(0, units), lane_block(k * 2 + 1 - y, 256)]
 
     def send_units(j, carry):
-        k = lax.rem(c + pick(j, (2, 1, 3, 0)), 4)
+        k = lax.rem(c + pick(j, (2, 3, 1, 0)), 4)
         unit_grads(k, 1 - y)
         wires.copy(u_id + k, half_grads(k), unit_in.at[k], across).start()
         return carry
@@ -1245,7 +1245,7 @@
     lax.fori_loop(2, 4, send_units, 0)
 
     def keep_units(j, carry):
-        unit_grads(lax.rem(c + pick(j, (2, 1, 3, 0)), 4), y)
+        unit_grads(lax.rem(c + pick(j, (2, 3, 1, 0)), 4), y)
         return carry
 
     lax.fori_loop(0, 2, keep_units, 0)
@@ -1381,10 +1381,7 @@
 
         lax.fori_loop(0, 8, step, 0)
 
-    def q_sums(where, scratches):
-        def done(r, value):
-            gq_out[r, where] = value
-
+    def q_sums(where, scratches, done):
         return plane_scatter(
             wires, pos,
             lambda k, yy: q_block(gy_all, k * 2 + yy, where),
@@ -1392,9 +1389,16 @@
             gq_out.shape[0], scratches, done,
         )
 
+    def done_first(r, value):
+        gq_out[r] = value
+
+    def done_rest(r, value):
+        gk_out[r] = value[:, :n_key]
+        gv_out[r] = value[:, n_key:]
+
     first, rest = slice(0, n_query), slice(n_query, n_query + 2 * n_key)
     q_grad(1 - e, gy_all, first)
-    queries = [q_sums(first, s_q)]
+    queries = [q_sums(first, s_q, done_first)]
     advance(queries)
     q_grad(e, gq_part, first)
     advance(queries, 4)
@@ -1409,7 +1413,7 @@
     gqkv[:, n_query : n_query + n_key] = key_grads.astype(low)
     gqkv[:, n_query + n_key :] = total[:, n_key:].astype(low)
     q_grad(1 - e, gy_all, rest)
-    others = [q_sums(rest, s_k)]
+    others = [q_sums(rest, s_k, done_rest)]
     advance(others)
     q_grad(e, gq_part, rest)
     load_qkv.wait()
@@ -1493,7 +1497,9 @@
             shape((tokens, width), low),
             shape((tokens, width), wide),
             shape((3, units * 8, lanes), low),
-            shape((lanes, n_all), wide),
+            shape((lanes, n_query), wide),
+            shape((lanes, n_rest // 2), wide),
+            shape((lanes, n_rest // 2), wide),
             shape((n_query, lanes), wide),
             shape((8, lanes), wide),
             shape((width, n_all), low),
@@ -1502,16 +1508,10 @@
         in_specs=[pl.BlockSpec(memory_space=pltpu.MemorySpace.SMEM), pl.BlockSpec(memory_space=VMEM)]
         + [pl.BlockSpec(memory_space=HBM)] * 5
         + [pl.BlockSpec(memory_space=VMEM)] * 2,
-        out_specs=[
-            pl.BlockSpec(memory_space=VMEM),
-            pl.BlockSpec(memory_space=VMEM),
-            pl.BlockSpec(memory_space=HBM),
-            pl.BlockSpec(memory_space=VMEM),
-            pl.BlockSpec(memory_space=VMEM),
-            pl.BlockSpec(memory_space=VMEM),
-            pl.BlockSpec(memory_space=HBM),
-            pl.BlockSpec(memory_space=HBM),
-        ],
+        out_specs=[pl.BlockSpec(memory_space=VMEM)] * 2
+        + [pl.BlockSpec(memory_space=HBM)]
+        + [pl.BlockSpec(memory_space=VMEM)] * 5
+        + [pl.BlockSpec(memory_space=HBM)] * 2,
         scratch_shapes=[
             pltpu.SemaphoreType.DMA((320,)),
             pltpu.SemaphoreType.DMA((320,)),
@@ -1577,23 +1577,22 @@
     sine = jnp.tile(sine[:, 0], (1, 4)) * turn[None, :]
     valid = (positions < lengths[0])[:, None]
     grad_y = jnp.where(valid, cotangent[0], jnp.zeros((), low))
-    n_query, n_key = w_query.shape[1], key_matrix.shape[1]
     lanes = w_out.shape[1]
     qkv = jnp.concatenate([w_query, key_matrix, value_matrix], axis=1)
     gains = jnp.concatenate(
         [first_gain[None], second_gain[None], jnp.zeros((14, lanes), low)], axis=0
     )
     w3 = jnp.stack([w_gate.T, w_up.T, w_down])
-    layer_out, grad_states, g3, gq, go, gain, _, _ = layer_call(
+    layer_out, grad_states, g3, gq, gk, gv, go, gain, _, _ = layer_call(
         lengths, states[0], gains, qkv, w_out, w3, grad_y, cosine, sine
     )
     return (
         layer_out[None],
         grad_states[None],
         gain[0],
-        gq[:, :n_query],
-        gq[:, n_query : n_query + n_key],
-        gq[:, n_query + n_key :],
+        gq,
+        gk,
+        gv,
         go,
         gain[1],
         g3[0].T.astype(wide),

time: 325 us -> 323 us (level)
    slice x2 -> x0, local copies, waits for them, and re-layouts: 3.41 us -> none  [the longest x1 1.88 us: plane_shards(): gq[:, :n_query]]
    unnamed x19 -> x28, local copies, waits for them, and re-layouts: 6.35 us -> 8.41 us
where the time goes in v5:
time: 323 us; the launch traced here: 321 us
  Pallas kernels  299 us (93%)
  local copies, waits for them, and re-layouts  10.6 us (3%)
  other arithmetic  10.4 us (3%)
    pallas_call x1, Pallas kernels, layer_call(): pl.pallas_call(layer_kernel, name='layer', out_shape=(shape((tokens, widt...  299 us
    unnamed x28, local copies, waits for them, and re-layouts  8.41 us

profile of v5, /device:TPU:8, one launch (start us, length us, event | category | flops | bytes accessed | tf_op | source)
XLA Modules:
  0.0 321.2 jit_solution(8158230537025730894)
XLA Ops:
  0.6 0.0 copy-start.2
  0.7 0.0 copy-start.1
  1.5 0.1 pad.8.clone
  1.5 1.3 maximum_maximum_fusion.gains
  2.9 0.1 multiply_sine_fusion
  3.0 0.1 copy.29
  3.1 0.6 broadcast_multiply_fusion.sine
  3.8 0.7 copy.30.cosine
  4.5 1.8 pad_maximum_fusion.1.qkv
  6.3 1.9 bitcast_select_fusion.gy
  8.3 0.0 copy-done.1
  8.3 0.3 copy.27
  8.6 0.0 copy-done.2
  8.6 0.3 copy.28
  9.0 0.0 copy-done.3
  9.0 1.6 pad_maximum_fusion.w3
  10.6 298.7 %layer.1 = (bf16[128,2048]{1,0:T(8,128)(2,1)}, f32[128,2048]{1,0:T(8,128)}, bf16[3,2816,128]{2,1,0:T(8,128)(2,1)}, f32[128,1024]{1,0:T(8,128)}, f32[128,128]{1,0...) custom-call(s32[1]{0:T(128)} %copy.39.lengths, ...), custom_call_target="tpu_custom_call" | custom-call | tf_op jit(solution)/shard_map/layer/pallas_call | solution.py:1493
  309.2 1.3 slice_bitcast_fusion
  310.5 2.9 bitcast_convert_fusion
  313.4 1.5 copy.32
  315.0 1.5 copy.31
  316.5 0.0 copy-done.6
  316.5 0.0 copy-start.4
  316.5 0.8 copy.40
  317.3 0.0 copy-done
  317.3 1.0 copy.41
  318.3 0.0 copy-done.5
  318.3 0.8 copy.42
  319.1 0.6 copy.43
  319.7 0.6 copy.44
  320.4 0.0 copy-done.4
  320.4 0.8 copy.45
  (15 shorter events, 0.1 us)
Async XLA Ops:
  0.6 8.0 %copy-start.2 = (bf16[128,2816]{1,0:T(8,128)(2,1)S(1)}, bf16[128,2816]{1,0:T(8,128)(2,1)}, u32[]{:S(2)}) copy-start(bf16[128,2816]{1,0:T(8,128)(2,1)} %param.21) | copy-start | bytes 2162692
  0.7 7.6 %copy-start.1 = (bf16[128,2816]{1,0:T(8,128)(2,1)S(1)}, bf16[128,2816]{1,0:T(8,128)(2,1)}, u32[]{:S(2)}) copy-start(bf16[128,2816]{1,0:T(8,128)(2,1)} %param.20) | copy-start | bytes 2162692
  4.5 4.5 %copy-start.3 = (bf16[2816,128]{1,0:T(8,128)(2,1)S(1)}, bf16[2816,128]{1,0:T(8,128)(2,1)}, u32[]{:S(2)}) copy-start(bf16[2816,128]{1,0:T(8,128)(2,1)} %param.22) | copy-start | bytes 2162692
  315.0 1.5 copy-start.6
  315.0 2.4 copy-start
  316.5 1.8 copy-start.5
  316.5 2.6 copy-start.8
  316.5 3.2 %copy-start.7 = (f32[128,128]{1,0:T(8,128)S(1)}, f32[128,128]{1,0:T(8,128)}, u32[]{:S(2)}) copy-start(f32[128,128]{1,0:T(8,128)} %get-tuple-element.72) | copy-start | bytes 196612
  316.5 3.8 %copy-start.4 = (f32[1024,128]{1,0:T(8,128)S(1)}, f32[1024,128]{1,0:T(8,128)}, u32[]{:S(2)}) copy-start(f32[1024,128]{1,0:T(8,128)} %get-tuple-element.73) | copy-start | bytes 1572868
